TPU v7x, 128 devices: a whole 4x4x4 slice. The times are simulated.
128 devices in a mesh: off: 64 (over z, x, y), kx: 2 (over core).
Axes of the slice: x: 4, y: 4, z: 4, core: 2. Of those that a mesh axis runs over, the one named last changes fastest.
Arguments:
- traces: bfloat16 [65536, 1024], P(('off', 'kx')), may hold values from -6 to 6
- trace_offset: int32 [65536], P(('off', 'kx')), may hold values from 0 to 127, as said below
- trace_midpoint: int32 [65536], P(('off', 'kx')), may hold values from 0 to 1023
- trace_count: int32 [128], P(('off', 'kx')), may hold values from 128 to 512, as said below
- continuation_operator: bfloat16 [512, 2, 128, 128], P('off'), may hold values from -0.5 to 0.5
Outputs:
- continued: float32 [2, 512, 1024, 128], P(None, 'off', 'kx')
Inputs may be any that keep to these rules, and one draw needn't show every extreme that they name: `trace_offset`: only the first trace_count[d] rows of device d of off+kx are used. Among them at most 8 go to one owner (an offset of one index of off's 2 planes with a midpoint of one index of kx's 512 midpoints); in every draw some device sends 8 to some owner and some owner receives 8 from every device. `trace_count`: some device uses all its rows.
All inputs are finite; a program needn't handle non-finite values.
Results may differ from a plain program's by a relative error of at most 0.014.
Values may be sent and summed in bfloat16 or wider, within the bound.
A program may use at most 192 MiB of HBM per device.

v0:
```python
import math

import jax
import jax.numpy as jnp
from jax import lax
from jax.sharding import PartitionSpec as P

NOFF = 128
NM = 1024
CAP = 8


def wave_tables(wave_rows, mid_cols):
    phase = wave_rows[:, None] * mid_cols[None, :] % NM
    angle = phase.astype(jnp.float32) * (2.0 * math.pi / NM)
    return (jnp.cos(angle).astype(jnp.bfloat16), jnp.sin(angle).astype(jnp.bfloat16))


def apply_transform(tables, midpoint_rows, planes, freq_count):
    cosine, sine = tables
    along = jnp.dot(cosine, midpoint_rows, preferred_element_type=jnp.float32)
    across = jnp.dot(sine, midpoint_rows, preferred_element_type=jnp.float32)
    along = along.reshape(along.shape[0], planes, 2, freq_count)
    across = across.reshape(across.shape[0], planes, 2, freq_count)
    real_part = along[:, :, 0, :] + across[:, :, 1, :]
    imag_part = along[:, :, 1, :] - across[:, :, 0, :]
    return jnp.stack([real_part, imag_part], axis=2)


def midpoint_transform(midpoint_rows, planes, freq_count, mid_cells):
    column = lax.axis_index("kx")
    mid_cols = column * mid_cells + jnp.arange(mid_cells, dtype=jnp.int32)
    wave_rows = jnp.arange(lax.axis_size("kx") * mid_cells, dtype=jnp.int32)
    return lax.psum_scatter(
        apply_transform(wave_tables(wave_rows, mid_cols), midpoint_rows, planes, freq_count).astype(
            jnp.bfloat16
        ),
        "kx",
        scatter_dimension=0,
        tiled=True,
    ).astype(jnp.float32)


def shards(traces, trace_offset, trace_midpoint, trace_count, continuation_operator):
    off_devices = lax.axis_size("off")
    kx_devices = lax.axis_size("kx")
    owners = off_devices * kx_devices
    planes = NOFF // off_devices
    mid_cells = NM // kx_devices
    row_count = traces.shape[0]
    row_width = traces.shape[1]
    freq_count = row_width // 2
    position = jnp.arange(row_count, dtype=jnp.int32)
    live_rows = position < trace_count[0]
    target = trace_offset // planes * kx_devices + trace_midpoint // mid_cells
    marked = (
        (target[:, None] == jnp.arange(owners, dtype=jnp.int32)[None, :]) & live_rows[:, None]
    ).astype(jnp.int32)
    ranked = jnp.sum(jnp.cumsum(marked, axis=0) * marked, axis=1) - 1
    slot_total = owners * CAP
    placed = jnp.where(live_rows, target * CAP + ranked, slot_total)
    local_bin = trace_offset % planes * mid_cells + trace_midpoint % mid_cells
    outgoing = jnp.zeros((slot_total, row_width), jnp.bfloat16).at[placed].set(traces, mode="drop")
    labels = jnp.full((slot_total,), -1, jnp.int32).at[placed].set(local_bin, mode="drop")
    arrived, arrived_labels = (
        lax.all_to_all(outgoing, ("off", "kx"), split_axis=0, concat_axis=0, tiled=True),
        lax.all_to_all(labels, ("off", "kx"), split_axis=0, concat_axis=0, tiled=True),
    )
    cell_total = planes * mid_cells
    member = arrived_labels[None, :] == jnp.arange(cell_total, dtype=jnp.int32)[:, None]
    binned = jnp.dot(member.astype(jnp.bfloat16), arrived, preferred_element_type=jnp.float32)
    fold_count = jnp.sum(member.astype(jnp.float32), axis=1)
    stacked = (binned / jnp.maximum(fold_count, 1.0)[:, None]).astype(jnp.bfloat16)
    midpoint_rows = (
        stacked.reshape(planes, mid_cells, row_width)
        .transpose(1, 0, 2)
        .reshape(mid_cells, planes * row_width)
    )
    spectrum_sum = midpoint_transform(midpoint_rows, planes, freq_count, mid_cells)
    spectrum = spectrum_sum.astype(jnp.bfloat16)
    regrouped = lax.all_to_all(spectrum, "off", split_axis=3, concat_axis=1, tiled=True)
    real_part = regrouped[:, :, 0, :]
    imag_part = regrouped[:, :, 1, :]
    op_real = continuation_operator[:, 0]
    op_imag = continuation_operator[:, 1]
    cont_real = jnp.einsum(
        "fpo,kof->fkp", op_real, real_part, preferred_element_type=jnp.float32
    ) - jnp.einsum("fpo,kof->fkp", op_imag, imag_part, preferred_element_type=jnp.float32)
    cont_imag = jnp.einsum(
        "fpo,kof->fkp", op_real, imag_part, preferred_element_type=jnp.float32
    ) + jnp.einsum("fpo,kof->fkp", op_imag, real_part, preferred_element_type=jnp.float32)
    return jnp.stack([cont_real, cont_imag], axis=0)


def solution(mesh):
    in_specs = (
        P(("off", "kx"), None),
        P(("off", "kx")),
        P(("off", "kx")),
        P(("off", "kx")),
        P("off", None, None, None),
    )
    out_specs = P(None, "off", "kx", None)
    return jax.shard_map(shards, mesh=mesh, in_specs=in_specs, out_specs=out_specs, check_vma=False)
```

profile of v0, /device:TPU:1, one launch (start us, length us, event | category | flops | bytes accessed | tf_op | source)
XLA Modules:
  0.0 167.0 jit_solution(12931942341166037979)
XLA Ops:
  7.2 0.7 fusion.48
  7.9 0.1 copy.29
  8.1 0.3 fusion.34
  8.5 0.3 fusion.33
  8.8 2.4 %scatter_custom_fusion = s32[1024]{0:T(1024)S(1)} fusion(s32[512]{0:T(512)S(1)} %compare_select_fusion, s32[512]{0:T(512)S(1)} %get-tuple-element.9, s32[]{:T(128)} %constant.78.clone.1), kind=kCustom, calls=%fused_computation.80 | custom fusion | bytes 4100 | tf_op jit(solution)/shard_map/scatter | solution.py:64
  11.3 0.7 all_to_all.27
  12.0 11.5 %all-to-all-start = ((s32[128,8,1]{1,2,0:T(1,128)}), s32[128,8,1]{1,2,0:T(1,128)S(1)}, u32[]{:S(2)}, u32[]{:S(2)}) async-start(s32[128,8,1]{1,2,0:T(1,128)} %bitcast.7), calls=%async_computation | async-start | bytes 131072 | tf_op jit(solution)/shard_map/all_to_all | solution.py:67
  23.5 4.8 %scatter_custom_fusion.1 = bf16[1024,1024]{1,0:T(8,128)(2,1)} fusion(s32[512]{0:T(512)S(1)} %compare_select_fusion, bf16[512,1024]{1,0:T(8,128)(2,1)} %param.5, bf16[]{:T(256)} %constant.85.clone.1), kind=kCustom, calls=%fused_computation.38 | custom fusion | bytes 2097664 | tf_op jit(solution)/shard_map/scatter | solution.py:63
  28.3 4.8 %all-to-all-done = s32[128,8,1]{1,2,0:T(1,128)S(1)} async-done(((s32[128,8,1]{1,2,0:T(1,128)}), s32[128,8,1]{1,2,0:T(1,128)S(1)}, u32[]{:S(2)}, u32[]{:S(2)}) %all-to-all-start) | async-done | bytes 4128 | tf_op jit(solution)/shard_map/all_to_all | solution.py:67
  33.1 4.9 %all-to-all-start.1 = ((bf16[128,8,1024]{2,1,0:T(8,128)(2,1)}), bf16[128,8,1024]{2,1,0:T(8,128)(2,1)S(1)}, u32[]{:S(2)}, u32[]{:S(2)}) async-start(bf16[128,8,1024]{2,1,0:T(8,128)(2,1)} %bitcast.8), calls=%async_computation.1 | async-start | bytes 4194304 | tf_op jit(solution)/shard_map/all_to_all | solution.py:66
  38.0 0.0 reduce-scatter.2.cloned.1.call-start
  38.1 0.6 broadcast.105
  38.7 0.8 reduce.3
  39.6 0.1 eq.50
  39.7 0.5 convert_reduce_fusion
  40.2 28.4 %all-to-all-done.1 = bf16[128,8,1024]{2,1,0:T(8,128)(2,1)S(1)} async-done(((bf16[128,8,1024]{2,1,0:T(8,128)(2,1)}), bf16[128,8,1024]{2,1,0:T(8,128)(2,1)S(1)}, u32[]{:S(2)}, u32[]{:S(2)}) %all-to-all-start.1) | async-done | bytes 2097184 | tf_op jit(solution)/shard_map/all_to_all | solution.py:66
  68.6 3.7 %divide_convert_fusion = bf16[1024,1024]{1,0:T(8,128)(2,1)} fusion(f32[1024]{0:T(1024)S(1)} %broadcast_maximum_fusion, bf16[128,8,1024]{2,1,0:T(8,128)(2,1)S(1)} %all-to-all-done.1, s32[1024]{0:T(1024)S(1)} %eq.50), kind=kOutput, calls=%fused_computation.8 | convolution fusion | flops 2150629376 | bytes 4202496 | tf_op jit(solution)/shard_map/dot_general | solution.py:71
  72.2 3.0 %copy.32 = bf16[2,512,1024]{1,2,0:T(8,128)(2,1)S(1)} copy(bf16[2,512,1024]{2,1,0:T(8,128)(2,1)} %bitcast.82) | data formatting | bytes 4194304 | tf_op jit(solution)/shard_map/reshape | solution.py:75
  75.3 9.5 %fusion.17 = f32[1024,2,2,512]{3,0,2,1:T(8,128)S(1)} fusion(bf16[2,2,512,512]{3,2,1,0:T(8,128)(2,1)S(1)} %bitcast.83, s32[512]{0:T(512)S(1)} %iota_add_fusion), kind=kOutput, calls=%fused_computation.31 | convolution fusion | flops 2155347968 | bytes 10487808 | tf_op jit(solution)/shard_map/dot_general | solution.py:22
  84.8 9.7 %fusion.14 = f32[1024,2,2,512]{3,0,2,1:T(8,128)S(1)} fusion(bf16[2,2,512,512]{3,2,1,0:T(8,128)(2,1)S(1)} %bitcast.84, s32[512]{0:T(512)S(1)} %iota_add_fusion), kind=kOutput, calls=%fused_computation.29 | convolution fusion | flops 2155347968 | bytes 10487808 | tf_op jit(solution)/shard_map/dot_general | solution.py:21
  94.4 1.7 fusion.1
  96.1 2.4 %pad_maximum_fusion = bf16[1024,2,2,512]{3,0,2,1:T(8,128)(2,1)} fusion(bf16[1024,2,1,512]{3,0,2,1:T(8,128)(2,1)S(1)} %get-tuple-element.6, bf16[1024,2,1,512]{3,0,2,1:T(8,128)(2,1)S(1)} %get-tuple-element.5), kind=kLoop, calls=%fused_computation.6 | loop fusion | flops 2097152 | bytes 8388608 | tf_op jit(solution)/shard_map/stack | solution.py:27
  98.5 0.0 reduce-scatter.2.cloned.1.call-update
  98.5 10.5 %reduce-scatter.2.cloned.1.call-done = bf16[512,2,2,512]{3,0,2,1:T(8,128)(2,1)} async-done(((bf16[1024,2,2,512]{3,0,2,1:T(8,128)(2,1)}), bf16[512,2,2,512]{3,0,2,1:T(8,128)(2,1)}) %reduce-scatter.2.cloned.1.call-update) | async-done | bytes 2097168 | tf_op jit(solution)/shard_map/reduce_scatter | solution.py:34
  109.0 4.9 %copy.33 = bf16[512,2,2,512]{0,2,1,3:T(2,128)(2,1)S(1)} copy(bf16[512,2,2,512]{3,0,2,1:T(8,128)(2,1)} %reduce-scatter.2.cloned.1.call-done) | data formatting | bytes 4194304 | tf_op jit(solution)/shard_map/reduce_scatter | solution.py:34
  114.0 38.1 %all_to_all.39 = bf16[512,2,2,512]{0,2,1,3:T(2,128)(2,1)S(1)} all-to-all(bf16[512,2,2,512]{0,2,1,3:T(2,128)(2,1)S(1)} %copy.33), channel_id=1, replica_groups=mesh['off'=64,'kx'=2] {'off'}, dimensions={3} | all-to-all | bytes 4194304 | tf_op jit(solution)/shard_map/all_to_all | solution.py:81
  152.1 0.4 copy.47
  152.5 0.3 copy.35
  152.8 0.2 fusion.61
  153.0 1.0 copy.42
  154.0 1.0 copy.44
  155.0 0.0 copy-start
  155.0 1.4 fusion.19
  156.5 0.0 copy-done
  156.5 0.4 fusion.23
  156.9 0.5 add_bitcast_fusion
  157.4 0.5 subtract_bitcast_fusion
  157.8 2.3 %pad_maximum_fusion.1 = f32[2,8,512,128]{3,2,1,0:T(8,128)} fusion(f32[1,8,512,128]{3,2,1,0:T(8,128)S(1)} %add_bitcast_fusion, f32[1,8,512,128]{3,2,1,0:T(8,128)S(1)} %subtract_bitcast_fusion), kind=kLoop, calls=%fused_computation.7 | loop fusion | flops 1048576 | bytes 8388608 | tf_op jit(solution)/shard_map/stack | solution.py:92
  (11 shorter events, 0.1 us)
Async XLA Ops:
  12.0 21.1 %all-to-all-start = ((s32[128,8,1]{1,2,0:T(1,128)}), s32[128,8,1]{1,2,0:T(1,128)S(1)}, u32[]{:S(2)}, u32[]{:S(2)}) async-start(s32[128,8,1]{1,2,0:T(1,128)} %bitcast.7), calls=%async_computation | async-start | bytes 131072 | tf_op jit(solution)/shard_map/all_to_all | solution.py:67
  33.1 35.5 %all-to-all-start.1 = ((bf16[128,8,1024]{2,1,0:T(8,128)(2,1)}), bf16[128,8,1024]{2,1,0:T(8,128)(2,1)S(1)}, u32[]{:S(2)}, u32[]{:S(2)}) async-start(bf16[128,8,1024]{2,1,0:T(8,128)(2,1)} %bitcast.8), calls=%async_computation.1 | async-start | bytes 4194304 | tf_op jit(solution)/shard_map/all_to_all | solution.py:66
  38.0 71.0 %reduce-scatter.2.cloned.1.call-start = ((), (), s32[]{:S(2)}) async-start(), calls=%async_computation.4 | async-start | bytes 6291456 | tf_op jit(solution)/shard_map/reduce_scatter | solution.py:34
  155.0 1.5 copy-start
Sparse Core Ops, SparseCore 0:
  98.6 10.3 reduce-scatter.1
where the time goes:
time: 168 us; the launch traced here: 167 us
  waiting for transfers between devices  43.8 us (26%)
  blocking collectives  38.1 us (23%)
  matrix products  25.6 us (15%)
  local copies, waits for them, and re-layouts  19.6 us (12%)
  starting transfers between devices  16.5 us (10%)
  between operations  14.3 us (9%)
  other arithmetic  9.12 us (5%)
    all_to_all x1, blocking collectives, shards(): lax.all_to_all(spectrum, 'off', split_axis=3, concat_axis=1, tiled=True)  38.1 us
    all_to_all x1, waiting for transfers between devices, shards(): lax.all_to_all(outgoing, ('off', 'kx'), split_axis=0, concat_axis=0, tile...  28.4 us
    all_to_all x1, starting transfers between devices, shards(): lax.all_to_all(labels, ('off', 'kx'), split_axis=0, concat_axis=0, tiled=...  11.5 us
    reduce_scatter x1, waiting for transfers between devices, midpoint_transform(): lax.psum_scatter(apply_transform(wave_tables(wave_rows, mid_cols), midpoi...  10.5 us
    dot_general x1, matrix products, apply_transform(): along = jnp.dot(cosine, midpoint_rows, preferred_element_type=jnp.float32)  9.67 us
    dot_general x1, matrix products, apply_transform(): across = jnp.dot(sine, midpoint_rows, preferred_element_type=jnp.float32)  9.5 us
    all_to_all x1, starting transfers between devices, shards(): lax.all_to_all(outgoing, ('off', 'kx'), split_axis=0, concat_axis=0, tile...  4.95 us
    reduce_scatter x1, local copies, waits for them, and re-layouts, midpoint_transform(): lax.psum_scatter(apply_transform(wave_tables(wave_rows, mid_cols), midpoi...  4.94 us
  transfers between devices with their start and end apart: 3, of which 3 were waited for; matrix products, arithmetic and copies ran while one was open for 4% of the time, Pallas kernels for 0%

commit v1 on v0

v1 whole, which is shorter than its diff:
```python
import functools

import jax
import jax.numpy as jnp
import numpy as np
from jax import lax
from jax.experimental import pallas as pl
from jax.experimental.pallas import tpu as pltpu
from jax.sharding import PartitionSpec as P

NOFF = 128
NM = 1024
NF = 512
CAP = 8
OFFS = 64
OWNERS = 128
HALF = 64
SLOTS = OWNERS * CAP
BF = jnp.bfloat16
F32 = jnp.float32

VMEM_SPEC = pl.BlockSpec(memory_space=pltpu.VMEM)
ANY_SPEC = pl.BlockSpec(memory_space=pl.ANY)


def nt(a, b):
    return lax.dot_general(a, b, (((1,), (1,)), ((), ())), preferred_element_type=F32)


def wave_tables():
    k = np.arange(512)
    tables = []
    for par in range(2):
        m = np.concatenate(
            [h * 512 + b * 256 + np.arange(128) * 2 + par for h in range(2) for b in range(2)]
        )
        phase = (k[:, None] * m[None, :]) % NM
        angle = phase * (2.0 * np.pi / NM)
        tables.append(np.concatenate([np.cos(angle), np.sin(angle)], axis=1))
    return np.stack(tables).astype(np.float32)


def prep_kernel(slot_ref, traces_ref, out_ref):
    slot = slot_ref[...]
    place = (
        lax.broadcasted_iota(jnp.int32, (SLOTS, 512), 0) == jnp.broadcast_to(slot, (SLOTS, 512))
    ).astype(F32).astype(BF)

    def part(j, _):
        lanes = pl.multiple_of(j * 128, 128)
        res = []
        for ri in range(2):
            cols = traces_ref[:, pl.ds(ri * NF + lanes, 128)]
            res.append(
                lax.dot_general(cols, place, (((0,), (1,)), ((), ())), preferred_element_type=F32)
            )
        for g in range(16):
            block = jnp.concatenate(
                [res[0][g * 8 : g * 8 + 8], res[1][g * 8 : g * 8 + 8]], axis=0
            ).astype(BF)
            out_ref[j * 16 + g, 0] = block[:, :512]
            out_ref[j * 16 + g, 1] = block[:, 512:]
        return 0

    lax.fori_loop(0, 4, part, 0)


def prepare(slot, traces):
    return pl.pallas_call(
        prep_kernel,
        out_shape=jax.ShapeDtypeStruct((OFFS, 2, 16, 512), BF),
        in_specs=[VMEM_SPEC, VMEM_SPEC],
        out_specs=VMEM_SPEC,
        compiler_params=pltpu.CompilerParams(vmem_limit_bytes=48 << 20),
    )(slot, traces)


def regroup(parts):
    lane = lax.broadcasted_iota(jnp.int32, parts[0].shape, 1) // CAP
    parts = list(parts)
    for b in range(4):
        sh = CAP << b
        low = (lane >> b) % 2 == 0
        new = list(parts)
        for i in range(16):
            if (i >> b) & 1 == 0:
                j = i | (1 << b)
                new[i] = jnp.where(low, parts[i], jnp.roll(parts[j], sh, axis=1))
                new[j] = jnp.where(low, jnp.roll(parts[i], -sh, axis=1), parts[j])
        parts = new
    return parts


def bin_kernel(core, rows_ref, meta_ref, table_ref, own_ref, send_ref, y_ref, mm_ref, left_ref, hot_ref, s32_ref, s16_ref):
    def by_owner(i, _):
        sg, col = i // 4, i % 4
        lanes = pl.multiple_of(col * 128, 128)
        got = regroup([rows_ref[s * 8 + sg, :, pl.ds(lanes, 128)] for s in range(16)])
        for w in range(16):
            y_ref[col * 16 + w, :, pl.ds(pl.multiple_of(sg * 128, 128), 128)] = got[w]
        return 0

    lax.fori_loop(0, 32, by_owner, 0)

    def meta_by_owner(col, _):
        lanes = pl.multiple_of(col * 128, 128)
        got = regroup([meta_ref[s, :, pl.ds(lanes, 128)] for s in range(16)])
        for w in range(16):
            mm_ref[col * 16 + w] = got[w].astype(F32)
        return 0

    lax.fori_loop(0, 4, meta_by_owner, 0)

    def one_owner(w, _):
        pair, h = w // 2, w % 2
        meta = mm_ref[w]
        row_id = lax.broadcasted_iota(jnp.int32, (128, 128), 0).astype(F32).astype(BF)
        one = jnp.ones((), BF)
        zero = jnp.zeros((), BF)
        for sg in range(8):
            lanes = slice(sg * 128, sg * 128 + 128)
            combo = jnp.broadcast_to(meta[2 * sg : 2 * sg + 1], (16, 128)).astype(BF)
            low = jnp.broadcast_to(meta[2 * sg + 1 : 2 * sg + 2], (128, 128)).astype(BF)
            data = y_ref[w, :, lanes]
            for q in range(8):
                left_ref[q * 16 : q * 16 + 16, lanes] = jnp.where(
                    combo == jnp.asarray(q, BF), data, zero
                )
            left_ref[128:144, lanes] = jnp.where(combo == row_id[:16], one, zero)
            hot_ref[:, lanes] = jnp.where(low == row_id, one, zero)
        cells = nt(left_ref[...], hot_ref[...])
        fold = jnp.maximum(cells[128:136], 1.0)
        for q in range(8):
            o2, par, b8 = q // 4, (q // 2) % 2, q % 2
            mean = cells[q * 16 : q * 16 + 16] / fold[q : q + 1]
            cells_of = s32_ref.at[par * 4 + h * 2 + b8]
            row = pair * 2 + o2
            cells_of[pl.ds(row, 8, stride=128), :] = mean[:8]
            cells_of[pl.ds(64 + row, 8, stride=128), :] = mean[8:]
        return 0

    lax.fori_loop(0, HALF, one_owner, 0)

    def to_bf16(f, _):
        r0 = pl.multiple_of(f * 128, 128)
        for lb in range(8):
            par, lane0 = lb // 4, (lb % 4) * 128
            re = s32_ref[lb, pl.ds(r0, 64), :].astype(BF)
            im = s32_ref[lb, pl.ds(r0 + 64, 64), :].astype(BF)
            s16_ref[par, pl.ds(r0, 64), lane0 : lane0 + 128] = re
            s16_ref[par, pl.ds(r0 + 64, 64), lane0 : lane0 + 128] = im
            s16_ref[par, pl.ds(r0, 64), 512 + lane0 : 640 + lane0] = im
            s16_ref[par, pl.ds(r0 + 64, 64), 512 + lane0 : 640 + lane0] = -re
        return 0

    lax.fori_loop(0, 8, to_bf16, 0)
    sign = (1 - 2 * core).astype(F32)

    def transform(f, _):
        r0 = pl.multiple_of(f * 256, 256)
        even = nt(table_ref[0], s16_ref[0, pl.ds(r0, 256), :])
        odd = nt(table_ref[1], s16_ref[1, pl.ds(r0, 256), :]) * sign
        own_ref[:, pl.ds(r0, 256)] = (even + odd).astype(BF)
        send_ref[:, pl.ds(r0, 256)] = (even - odd).astype(BF)
        return 0

    lax.fori_loop(0, 4, transform, 0)


def bin_and_transform(rows, meta, table):
    half = jax.ShapeDtypeStruct((512, 1024), BF)

    def kernel(*refs):
        bin_kernel(lax.axis_index("kx"), *refs)

    return pl.pallas_call(
        kernel,
        out_shape=(half, half),
        in_specs=[VMEM_SPEC] * 3,
        out_specs=(VMEM_SPEC, VMEM_SPEC),
        scratch_shapes=[
            pltpu.VMEM((HALF, 16, 1024), BF),
            pltpu.VMEM((HALF, 16, 128), F32),
            pltpu.VMEM((144, 1024), BF),
            pltpu.VMEM((128, 1024), BF),
            pltpu.VMEM((8, 1024, 128), F32),
            pltpu.VMEM((2, 1024, 1024), BF),
        ],
        compiler_params=pltpu.CompilerParams(vmem_limit_bytes=56 << 20),
    )(rows, meta, table)


def mix_kernel(first_ref, second_ref, op_ref, out_ref):
    for ri in range(2):
        pass
    z = jnp.concatenate([first_ref[...], second_ref[...]], axis=1)
    res = nt(z, op_ref[0])
    out_ref[0, 0] = res[:, :128]
    out_ref[1, 0] = res[:, 128:]


def mix(first, second, op):
    return pl.pallas_call(
        mix_kernel,
        out_shape=jax.ShapeDtypeStruct((2, 8, 512, 128), F32),
        grid=(8,),
        in_specs=[
            pl.BlockSpec((512, 128), lambda f: (0, f)),
            pl.BlockSpec((512, 128), lambda f: (0, f)),
            pl.BlockSpec((1, 256, 256), lambda f: (f, 0, 0)),
        ],
        out_specs=pl.BlockSpec((2, 1, 512, 128), lambda f: (0, f, 0, 0)),
        compiler_params=pltpu.CompilerParams(vmem_limit_bytes=40 << 20),
    )(first, second, op)


def shards(traces, trace_offset, trace_midpoint, trace_count, operator, table):
    core = lax.axis_index("kx")
    position = jnp.arange(512, dtype=jnp.int32)
    live = position < trace_count[0]
    owner = (trace_offset // 2) * 2 + trace_midpoint // 512
    marked = ((owner[:, None] == jnp.arange(OWNERS)[None, :]) & live[:, None]).astype(jnp.int32)
    rank = jnp.sum(jnp.cumsum(marked, axis=0) * marked, axis=1) - 1
    slot = jnp.where(live, owner * CAP + rank, SLOTS)
    combo = (trace_offset % 2) * 4 + (trace_midpoint % 2) * 2 + (trace_midpoint // 256) % 2
    low = (trace_midpoint % 256) // 2
    fields = jnp.stack([combo, low]).astype(F32)
    hot = (slot[:, None] == jnp.arange(SLOTS)[None, :]).astype(BF)
    coded = jnp.dot(fields.astype(BF), hot, preferred_element_type=F32)
    filled = jnp.sum(hot.astype(F32), axis=0)
    coded = jnp.where(filled > 0, coded, 255.0).astype(BF)

    outgoing = prepare(slot[None, :], traces).reshape(OWNERS, 16, 512)
    meta = lax.all_gather(coded, ("off", "kx"))
    meta = lax.dynamic_slice_in_dim(meta, core * 512, 512, axis=2).reshape(16, 16, 512)
    rows = lax.all_to_all(outgoing, ("off", "kx"), split_axis=0, concat_axis=0, tiled=True)
    own, send = bin_and_transform(rows, meta, table)
    other = lax.ppermute(send, "kx", [(0, 1), (1, 0)])
    first = jnp.where(core == 0, own, other)
    second = jnp.where(core == 0, other, own)

    re, im = operator[:, 0], operator[:, 1]
    op = jnp.stack([jnp.stack([re, -im], axis=2), jnp.stack([im, re], axis=2)], axis=1)
    op = op.reshape(8, 2, 128, 2, 2, HALF).transpose(0, 1, 2, 4, 3, 5).reshape(8, 256, 256)
    return mix(first, second, op)


def solution(mesh):
    def run(traces, trace_offset, trace_midpoint, trace_count, operator):
        table = jnp.asarray(wave_tables(), BF)
        return jax.shard_map(
            shards,
            mesh=mesh,
            in_specs=(
                P(("off", "kx"), None),
                P(("off", "kx")),
                P(("off", "kx")),
                P(("off", "kx")),
                P("off", None, None, None),
                P(),
            ),
            out_specs=P(None, "off", "kx", None),
            check_vma=False,
        )(traces, trace_offset, trace_midpoint, trace_count, operator, table)

    return run
```

time: 168 us -> 129 us (0.77)
  Pallas kernels: 0 us -> 52.4 us
  waiting for transfers between devices: 43.8 us -> 0.01 us
  matrix products: 25.6 us -> 0.52 us
  blocking collectives: 38.1 us -> 53.9 us
  local copies, waits for them, and re-layouts: 19.6 us -> 5.76 us
  between operations: 14.3 us -> 0.9 us
  other arithmetic: 9.12 us -> 3.58 us
  starting transfers between devices: 16.5 us -> 11.7 us
    all_gather x0 -> x1, blocking collectives: none -> 53.9 us  [shards(): meta = lax.all_gather(coded, ('off', 'kx'))]
    pallas_call x0 -> x3, Pallas kernels: none -> 52.4 us  [the longest x1 42.5 us: bin_and_transform(): pl.pallas_call(kernel, out_shape=(half, half), in_specs=[VMEM_SPEC] * 3,...]
    all_to_all x1 -> x0, blocking collectives: 38.1 us -> none  [shards(): lax.all_to_all(spectrum, 'off', split_axis=3, concat_axis=1, tiled=True)]
    all_to_all x1, waiting for transfers between devices: 28.4 us -> 0.01 us  [shards(): lax.all_to_all(outgoing, ('off', 'kx'), split_axis=0, concat_axis=0, tile...]
    dot_general x7 -> x1, matrix products: 25.6 us -> 0.52 us  [shards(): coded = jnp.dot(fields.astype(BF), hot, preferred_element_type=F32)]
    all_to_all x1 -> x0, starting transfers between devices: 11.5 us -> none  [shards(): lax.all_to_all(labels, ('off', 'kx'), split_axis=0, concat_axis=0, tiled=...]
    reduce_scatter x1 -> x0, waiting for transfers between devices: 10.5 us -> none  [midpoint_transform(): lax.psum_scatter(apply_transform(wave_tables(wave_rows, mid_cols), midpoi...]
    scatter x2 -> x0, local copies, waits for them, and re-layouts: 7.24 us -> none  [the longest x1 4.79 us: shards(): jnp.zeros((slot_total, row_width), jnp.bfloat16).at[placed]]
  transfers between devices with their start and end apart: 3 -> 2, of which waited for: 3 -> 0; matrix products, arithmetic and copies ran while one was open for 4% -> 4% of each run, Pallas kernels for 0% -> 0%
where the time goes in v1:
time: 129 us
  blocking collectives  53.9 us (42%)
  Pallas kernels  52.4 us (41%)
  starting transfers between devices  11.7 us (9%)
  local copies, waits for them, and re-layouts  5.76 us (4%)
  other arithmetic  3.58 us (3%)
    all_gather x1, blocking collectives, shards(): meta = lax.all_gather(coded, ('off', 'kx'))  53.9 us
    pallas_call x1, Pallas kernels, bin_and_transform(): pl.pallas_call(kernel, out_shape=(half, half), in_specs=[VMEM_SPEC] * 3,...  42.5 us
    all_to_all x1, starting transfers between devices, shards(): lax.all_to_all(outgoing, ('off', 'kx'), split_axis=0, concat_axis=0, tile...  11.5 us
    pallas_call x1, Pallas kernels, prepare(): pl.pallas_call(prep_kernel, out_shape=jax.ShapeDtypeStruct((OFFS, 2, 16,...  4.99 us
    pallas_call x1, Pallas kernels, mix(): pl.pallas_call(mix_kernel, out_shape=jax.ShapeDtypeStruct((2, 8, 512, 128...  4.89 us
    reshape x2, local copies, waits for them, and re-layouts, shards(): op.reshape(8, 2, 128, 2, 2, HALF).transpose(0, 1, 2, 4, 3, 5)  2.88 us
  transfers between devices with their start and end apart: 2, of which 0 were waited for; matrix products, arithmetic and copies ran while one was open for 4% of the time, Pallas kernels for 0%

profile of v1, /device:TPU:1, one launch (start us, length us, event | category | flops | bytes accessed | tf_op | source)
XLA Modules:
  0.0 128.7 jit_solution(12584202581216414085)
XLA Ops:
  0.0 0.0 copy-start
  0.8 0.7 fusion.20
  1.5 0.1 copy.23
  1.6 0.3 fusion.7
  2.1 0.3 fusion.6
  2.4 0.0 copy-done
  2.4 5.0 %shard_map.64 = bf16[64,2,16,512]{3,2,1,0:T(8,128)(2,1)} custom-call(s32[1,512]{1,0:T(1,128)S(1)} %bitcast.26, bf16[512,1024]{1,0:T(8,128)(2,1)S(1)} %copy-done), custom_call_target="tpu_custom_call" | custom-call | tf_op jit(solution)/shard_map/pallas_call | solution.py:69
  7.4 11.5 %all-to-all-start = ((bf16[128,16,512]{2,1,0:T(8,128)(2,1)}), bf16[128,16,512]{2,1,0:T(8,128)(2,1)S(1)}, u32[]{:S(2)}, u32[]{:S(2)}) async-start(bf16[128,16,512]{2,1,0:T(8,128)(2,1)} %bitcast.6), calls=%async_computation | async-start | bytes 4194304 | tf_op jit(solution)/shard_map/all_to_all | solution.py:236
  18.9 0.3 convert_reduce_fusion
  19.2 0.5 fusion.4
  19.7 53.9 %all-gather.1 = bf16[128,2,1024]{2,1,0:T(2,128)(2,1)S(1)} all-gather(bf16[1,2,1024]{2,1,0:T(2,128)(2,1)S(1)} %fusion.4), channel_id=2, replica_groups=mesh['off'=64,'kx'=2] {'off','kx'}, dimensions={0}, use_global_device_ids=true | all-gather | bytes 528384 | tf_op jit(solution)/shard_map/all_gather | solution.py:234
  73.6 0.2 constant_dynamic-slice_fusion
  73.8 0.8 reshape.61.refs_1_
  74.6 0.0 copy-start.2
  74.6 0.0 all-to-all-done.refs_0_
  74.6 0.0 copy-start.1
  74.6 1.3 %copy-done.1 = bf16[128,16,512]{2,1,0:T(8,128)(2,1)} copy-done((bf16[128,16,512]{2,1,0:T(8,128)(2,1)}, bf16[128,16,512]{2,1,0:T(8,128)(2,1)S(1)}, u32[]{:S(2)}) %copy-start.1) | copy-done | bytes 2097176
  75.9 42.5 %shard_map.65 = (bf16[512,1024]{1,0:T(8,128)(2,1)}, bf16[512,1024]{1,0:T(8,128)(2,1)}) custom-call(bf16[128,16,512]{2,1,0:T(8,128)(2,1)} %copy-done.1, bf16[16,16,512]{2,1,0:T(8,128)(2,1)} %reshape.61.refs_1_, bf16[2,512,1024]{2,1,0:T(8,128)(2,1)} %constant.101.clone.refs_2_), custom_call_target="tpu_custom_call" | custom-call | tf_op jit(solution)/shard_map/pallas_call | solution.py:176
  118.4 0.2 collective-permute-start
  118.6 0.0 copy-done.2
  118.6 0.2 copy.32
  118.8 0.1 neg.11
  118.9 0.2 copy.31
  119.1 0.1 maximum_bitcast_fusion
  119.2 1.5 %copy.29 = bf16[8,2,128,2,2,64]{5,4,3,2,1,0:T(2,128)(2,1)S(1)} copy(bf16[8,2,128,2,2,64]{2,5,3,0,4,1:T(8,128)(2,1)S(1)} %maximum_bitcast_fusion) | data formatting | bytes 2097152 | tf_op jit(solution)/shard_map/reshape | solution.py:244
  120.7 1.4 %reshape.69.op_ref = bf16[8,256,256]{2,1,0:T(8,128)(2,1)S(1)} reshape(bf16[8,2,128,2,2,64]{5,4,3,2,1,0:T(2,128)(2,1)S(1)} %copy.29) | data formatting | bytes 2097152 | tf_op jit(solution)/shard_map/reshape | solution.py:244
  122.1 0.0 collective-permute-done
  122.1 1.7 %broadcast_select_fusion = (bf16[512,1024]{1,0:T(8,128)(2,1)S(1)}, bf16[512,1024]{1,0:T(8,128)(2,1)S(1)}) fusion(bf16[512,1024]{1,0:T(8,128)(2,1)} %collective-permute-done, bf16[512,1024]{1,0:T(8,128)(2,1)} %get-tuple-element.7, pred[]{:T(512)S(6)} %eq.45), kind=kLoop, calls=%fused_computation.9 | loop fusion | flops 1048576 | bytes 4194305 | tf_op jit(solution)/shard_map/jit(_where)/select_n | solution.py:240
  123.8 4.9 %shard_map.66 = f32[2,8,512,128]{3,2,1,0:T(8,128)} custom-call(bf16[512,1024]{1,0:T(8,128)(2,1)S(1)} %get-tuple-element.10.first_ref, bf16[512,1024]{1,0:T(8,128)(2,1)S(1)} %get-tuple-element.9.second_ref, bf16[8,256,256]{2,1,0:T(8,128)(2,1)S(1)} %reshape.69.op_ref), custom_call_target="tpu_custom_call" | custom-call | tf_op jit(solution)/shard_map/pallas_call | solution.py:203
  (11 shorter events, 0.2 us)
Async XLA Ops:
  0.0 2.4 %copy-start = (bf16[512,1024]{1,0:T(8,128)(2,1)S(1)}, bf16[512,1024]{1,0:T(8,128)(2,1)}, u32[]{:S(2)}) copy-start(bf16[512,1024]{1,0:T(8,128)(2,1)} %traces_ref.1) | copy-start | bytes 3145732
  7.4 67.2 %all-to-all-start = ((bf16[128,16,512]{2,1,0:T(8,128)(2,1)}), bf16[128,16,512]{2,1,0:T(8,128)(2,1)S(1)}, u32[]{:S(2)}, u32[]{:S(2)}) async-start(bf16[128,16,512]{2,1,0:T(8,128)(2,1)} %bitcast.6), calls=%async_computation | async-start | bytes 4194304 | tf_op jit(solution)/shard_map/all_to_all | solution.py:236
  74.6 44.0 %copy-start.2 = (bf16[8,2,128,128]{3,2,1,0:T(8,128)(2,1)S(1)}, bf16[8,2,128,128]{3,2,1,0:T(8,128)(2,1)}, u32[]{:S(2)}) copy-start(bf16[8,2,128,128]{3,2,1,0:T(8,128)(2,1)} %param.10) | copy-start | bytes 1572868
  74.6 1.3 %copy-start.1 = (bf16[128,16,512]{2,1,0:T(8,128)(2,1)}, bf16[128,16,512]{2,1,0:T(8,128)(2,1)S(1)}, u32[]{:S(2)}) copy-start(bf16[128,16,512]{2,1,0:T(8,128)(2,1)S(1)} %all-to-all-done.refs_0_) | copy-start | bytes 6291460
  118.4 3.7 %collective-permute-start = (bf16[512,1024]{1,0:T(8,128)(2,1)}, bf16[512,1024]{1,0:T(8,128)(2,1)}, u32[]{:S(2)}, u32[]{:S(2)}) collective-permute-start(bf16[512,1024]{1,0:T(8,128)(2,1)} %get-tuple-element.8), channel_id=1, source_target_pairs={{0,1},{1,0},{2,3},{3,2},{4,5},{5,4},{6,7},{7,6},{8,9},{9,8},{10,11... | collective-permute-start | bytes 3145736 | tf_op jit(solution)/shard_map/ppermute | solution.py:238

commit v2 on v1

v2 whole, which is shorter than its diff:
```python
import jax
import jax.numpy as jnp
import numpy as np
from jax import lax
from jax.experimental import pallas as pl
from jax.experimental.pallas import tpu as pltpu
from jax.sharding import PartitionSpec as P

NM = 1024
NF = 512
CAP = 8
ROWS = 512
CHIPS = 64
HALF = 64
BF = jnp.bfloat16
F32 = jnp.float32
I32 = jnp.int32
MESH = pl.DeviceIdType.MESH

VMEM_SPEC = pl.BlockSpec(memory_space=pltpu.VMEM)
ANY_SPEC = pl.BlockSpec(memory_space=pl.ANY)


def nt(a, b):
    return lax.dot_general(a, b, (((1,), (1,)), ((), ())), preferred_element_type=F32)


def wave_tables():
    k = np.arange(512)
    tables = []
    for par in range(2):
        m = np.concatenate(
            [h * 512 + b * 256 + np.arange(128) * 2 + par for h in range(2) for b in range(2)]
        )
        angle = (k[:, None] * m[None, :]) % NM * (2.0 * np.pi / NM)
        tables.append(np.concatenate([np.cos(angle), np.sin(angle)], axis=1))
    return np.stack(tables).astype(np.float32)


def shifted(off, r, i):
    z, x, y = off // 16, (off // 4) % 4, off % 4
    dx, dy = i // 4, i % 4
    dz = (r + 8 - dx - dy) % 4
    return ((z + dz) % 4) * 16 + ((x + dx) % 4) * 4 + (y + dy) % 4


def sort_rows(xy, off_ref, mid_ref, cnt_ref, traces_ref, blocks_ref, meta_ref):
    offset, mid = off_ref[...], mid_ref[...]
    t = lax.broadcasted_iota(I32, (1, ROWS), 1)
    live = t < jnp.broadcast_to(cnt_ref[...], (1, ROWS))
    owner = jnp.where(live, (offset // 2) * 2 + mid // 512, 1024)
    key = owner * ROWS + t

    position = jnp.zeros((128, ROWS), I32)
    start = jnp.zeros((128, ROWS), I32)
    for b in range(4):
        lanes = slice(b * 128, b * 128 + 128)
        key_col = jnp.broadcast_to(key[:, lanes], (128, 128)).T[:, :1]
        own_col = jnp.broadcast_to(owner[:, lanes], (128, 128)).T[:, :1]
        position += (key_col < key).astype(I32)
        start += (own_col < owner).astype(I32)
    position = jnp.sum(position, axis=0, keepdims=True)
    rank = position - jnp.sum(start, axis=0, keepdims=True)
    position = jnp.where(live, position, ROWS)
    slot = (owner // 16) * 128 + ((owner % 16 + xy) % 16) * CAP + rank
    slot = jnp.where(live, slot, -1)

    combo = (offset % 2) * 4 + (mid % 2) * 2 + (mid // 256) % 2 + 1
    low = (mid % 256) // 2
    fields = jnp.concatenate(
        [position % 128, low, combo, jnp.zeros((13, ROWS), I32)], axis=0
    ).astype(F32).astype(BF)
    hot = (lax.broadcasted_iota(I32, (1024, ROWS), 0) == slot).astype(F32).astype(BF)
    coded = nt(fields, hot)
    coded = coded[0:1] * 8.0 + coded[1:2] * 1024.0 + coded[2:3] * 131072.0
    coded = jnp.concatenate([coded[:, c * 128 : c * 128 + 128] for c in range(8)], axis=0)
    before = jnp.sum(
        (owner < lax.broadcasted_iota(I32, (8, ROWS), 0) * 16).astype(F32), axis=1, keepdims=True
    ).astype(I32)
    lane = lax.broadcasted_iota(I32, (8, 128), 1)
    part = before // 128 + (lane < before % 128).astype(I32)
    meta_ref[...] = coded.astype(I32) + part

    place = (lax.broadcasted_iota(I32, (ROWS, ROWS), 0) == position).astype(F32).astype(BF)

    def cut(j, _):
        lanes = pl.multiple_of(j * 128, 128)
        both = []
        for ri in range(2):
            cols = traces_ref[:, pl.ds(ri * NF + lanes, 128)]
            both.append(
                lax.dot_general(cols, place, (((0,), (1,)), ((), ())), preferred_element_type=F32)
            )
        for g in range(16):
            blocks_ref[j * 16 + g] = jnp.concatenate(
                [both[0][g * 8 : g * 8 + 8], both[1][g * 8 : g * 8 + 8]], axis=0
            ).astype(BF)
        return 0

    lax.fori_loop(0, 4, cut, 0)


def regroup(parts, lane_group):
    now = [parts[(-u) % 16] for u in range(16)]
    for b in range(4):
        bit = (lane_group >> b) % 2 == 1
        now = [jnp.where(bit, now[(u - (1 << b)) % 16], now[u]) for u in range(16)]
    return now


def main_kernel(
    off_ref, mid_ref, cnt_ref, traces_ref, table_hbm, own_ref, other_ref,
    blocks, meta_out, got, meta, ex, dx, y_ref, mm, left, hot, acc, s32, s16, table, give,
    send_sem, recv_sem, msend_sem, mrecv_sem, local_sem, mx_send, mx_recv, dx_send, dx_recv,
    sp_send, sp_recv, table_sem,
):
    off, core = lax.axis_index("off"), lax.axis_index("kx")
    xy = off % 16
    total = off // 16 + (off // 4) % 4 + off % 4
    me = (total % 4) * 16 + xy
    mate = (off, 1 - core)

    bar = pltpu.get_barrier_semaphore()

    def greet(n, _):
        peer = shifted(off, n // 16, n % 16)
        pl.semaphore_signal(bar, inc=1, device_id=(peer, core), device_id_type=MESH)
        return 0

    lax.fori_loop(1, CHIPS, greet, 0)
    pl.semaphore_signal(bar, inc=1, device_id=mate, device_id_type=MESH)
    load_table = pltpu.make_async_copy(table_hbm, table, table_sem)
    load_table.start()

    sort_rows(xy, off_ref, mid_ref, cnt_ref, traces_ref, blocks, meta_out)

    def meta_slot(which, n):
        return meta.at[pl.ds(pl.multiple_of(which * 512 + n * 8, 8), 8)]

    keep = pltpu.make_async_copy(blocks.at[off], got.at[me], local_sem.at[0])
    keep.start()
    keep_meta = pltpu.make_async_copy(meta_out, meta_slot(0, me), local_sem.at[1])
    keep_meta.start()
    pl.semaphore_wait(bar, CHIPS)

    def send_meta(n, _):
        peer = shifted(off, n // 16, n % 16)
        pltpu.make_async_remote_copy(
            meta_out, meta_slot(0, me), msend_sem, mrecv_sem, device_id=(peer, core), device_id_type=MESH
        ).start()
        return 0

    def send_block(n, _):
        peer = shifted(off, n // 16, n % 16)
        pltpu.make_async_remote_copy(
            blocks.at[peer], got.at[me], send_sem, recv_sem.at[n // 16],
            device_id=(peer, core), device_id_type=MESH,
        ).start()
        return 0

    lax.fori_loop(1, CHIPS, send_meta, 0)
    lax.fori_loop(1, CHIPS, send_block, 0)

    def clear(w, _):
        acc[w] = jnp.zeros((144, 128), F32)
        return 0

    lax.fori_loop(0, HALF, clear, 0)

    keep_meta.wait()
    others = meta.at[pl.ds(0, 63 * 8)]
    pltpu.make_async_remote_copy(others, others, msend_sem, mrecv_sem, device_id=mate, device_id_type=MESH).wait()
    pass_meta = pltpu.make_async_remote_copy(
        meta.at[pl.ds(0, 512)], meta.at[pl.ds(512, 512)], mx_send, mx_recv, device_id=mate, device_id_type=MESH
    )
    pass_meta.start()
    pass_meta.wait()

    group16 = lax.broadcasted_iota(I32, (16, 128), 1) // CAP
    group8 = lax.broadcasted_iota(I32, (8, 128), 1) // CAP

    def meta_by_owner(col, _):
        row = core * 4 + col
        parts = [meta[pl.ds(row + s * 8, 8, stride=128), :] for s in range(16)]
        for w, part in enumerate(regroup(parts, group8)):
            mm[col * 16 + w] = part
        return 0

    lax.fori_loop(0, 4, meta_by_owner, 0)

    def one_round(r, _):
        kind = (total + 4 - r) % 4
        base = kind * 16

        def arrived(n):
            part = got.at[pl.ds(0, n)]
            pltpu.make_async_remote_copy(
                part, part, send_sem, recv_sem.at[r], device_id=mate, device_id_type=MESH
            ).wait_recv()

        @pl.when(r == 0)
        def _():
            keep.wait()
            arrived(15)

        @pl.when(r > 0)
        def _():
            arrived(16)

        def expand(s, _):
            n = base + s
            code = meta[pl.ds(pl.multiple_of(n * 8, 8), 8), :]
            index = (code // 8) % 128
            part = code % 8
            x = [got[n, :, i * 128 : i * 128 + 128].astype(F32) for i in range(4)]
            for c in range(8):
                pick = jnp.broadcast_to(part[c : c + 1], (16, 128))
                src = x[min(c, 3)]
                for i in range(min(c, 3) - 1, -1, -1):
                    src = jnp.where(pick == i, x[i], src)
                at = jnp.broadcast_to(index[c : c + 1], (16, 128))
                out = jnp.take_along_axis(src, at, axis=1, mode="promise_in_bounds")
                ex[r, c // 4, s, :, (c % 4) * 128 : (c % 4) * 128 + 128] = out.astype(BF)
            return 0

        lax.fori_loop(0, 16, expand, 0, unroll=4)
        swap = pltpu.make_async_remote_copy(
            ex.at[r, 1 - core], dx.at[r], dx_send.at[r], dx_recv.at[r], device_id=mate, device_id_type=MESH
        )
        swap.start()

        def by_owner(which, col):
            lanes = pl.ds(pl.multiple_of(col * 128, 128), 128)
            if which == 0:
                parts = [ex[r, core, s, :, lanes] for s in range(16)]
            else:
                parts = [dx[r, s, :, lanes] for s in range(16)]
            for w, part in enumerate(regroup(parts, group16)):
                y_ref[col * 16 + w, :, which * 128 : which * 128 + 128] = part

        def own_cols(col, _):
            by_owner(0, col)
            return 0

        def mate_cols(col, _):
            by_owner(1, col)
            return 0

        lax.fori_loop(0, 4, own_cols, 0)
        swap.wait()
        lax.fori_loop(0, 4, mate_cols, 0)

        def four_owners(w4, _):
            row_id = lax.broadcasted_iota(I32, (128, 128), 0).astype(F32).astype(BF)
            one, zero = jnp.ones((), BF), jnp.zeros((), BF)
            for u in range(4):
                w = w4 * 4 + u
                for which in range(2):
                    lanes = slice(which * 128, which * 128 + 128)
                    code = mm[w, pl.ds(which * 4 + kind, 1), :]
                    combo = (code // 131072).astype(F32)
                    low = ((code // 1024) % 128).astype(F32)
                    combo = jnp.broadcast_to(combo, (16, 128)).astype(BF)
                    low = jnp.broadcast_to(low, (128, 128)).astype(BF)
                    data = y_ref[w, :, lanes]
                    for q in range(8):
                        left[u, q * 16 : q * 16 + 16, lanes] = jnp.where(
                            combo == jnp.asarray(q + 1, BF), data, zero
                        )
                    left[u, 128:144, lanes] = jnp.where(combo == row_id[:16] + one, one, zero)
                    hot[u, :, lanes] = jnp.where(low == row_id, one, zero)
                acc[w] += nt(left[u], hot[u])
            return 0

        lax.fori_loop(0, HALF // 4, four_owners, 0)
        return 0

    lax.fori_loop(0, 4, one_round, 0)
    sent = blocks.at[pl.ds(0, 63)]
    pltpu.make_async_remote_copy(
        sent, sent, send_sem, recv_sem.at[0], device_id=mate, device_id_type=MESH
    ).wait_send()

    def means(w, _):
        pair, h = w // 2, w % 2
        fold = jnp.maximum(acc[w, 128:136], 1.0)
        for q in range(8):
            o2, par, b8 = q // 4, (q // 2) % 2, q % 2
            mean = acc[w, q * 16 : q * 16 + 16] / fold[q : q + 1]
            cells_of = s32.at[par * 4 + h * 2 + b8]
            row = pair * 2 + o2
            cells_of[pl.ds(row, 8, stride=128), :] = mean[:8]
            cells_of[pl.ds(64 + row, 8, stride=128), :] = mean[8:]
        return 0

    lax.fori_loop(0, HALF, means, 0)

    load_table.wait()
    sign = (1 - 2 * core).astype(F32)

    def handing(j):
        lanes = pl.ds(pl.multiple_of(j * 256, 256), 256)
        return pltpu.make_async_remote_copy(
            give.at[:, lanes], other_ref.at[:, lanes], sp_send.at[j], sp_recv.at[j],
            device_id=mate, device_id_type=MESH,
        )

    def transform(j, _):
        for f in range(2):
            r0 = pl.multiple_of(j * 256 + f * 128, 128)
            for lb in range(8):
                par, lane0 = lb // 4, (lb % 4) * 128
                re = s32[lb, pl.ds(r0, 64), :].astype(BF)
                im = s32[lb, pl.ds(r0 + 64, 64), :].astype(BF)
                s16[par, pl.ds(r0, 64), lane0 : lane0 + 128] = re
                s16[par, pl.ds(r0 + 64, 64), lane0 : lane0 + 128] = im
                s16[par, pl.ds(r0, 64), 512 + lane0 : 640 + lane0] = im
                s16[par, pl.ds(r0 + 64, 64), 512 + lane0 : 640 + lane0] = -re
        r0 = pl.multiple_of(j * 256, 256)
        even = nt(table[0], s16[0, pl.ds(r0, 256), :])
        odd = nt(table[1], s16[1, pl.ds(r0, 256), :]) * sign
        own_ref[:, pl.ds(r0, 256)] = (even + odd).astype(BF)
        give[:, pl.ds(r0, 256)] = (even - odd).astype(BF)
        handing(j).start()
        return 0

    lax.fori_loop(0, 4, transform, 0)

    def handed(j, _):
        handing(j).wait()
        return 0

    lax.fori_loop(0, 4, handed, 0)


def spectra(offset, mid, count, traces, table):
    half = jax.ShapeDtypeStruct((512, 1024), BF)
    dma = pltpu.SemaphoreType.DMA
    return pl.pallas_call(
        main_kernel,
        out_shape=(half, half),
        in_specs=[VMEM_SPEC] * 4 + [ANY_SPEC],
        out_specs=(VMEM_SPEC, VMEM_SPEC),
        scratch_shapes=[
            pltpu.VMEM((CHIPS, 16, ROWS), BF),
            pltpu.VMEM((8, 128), I32),
            pltpu.VMEM((CHIPS, 16, ROWS), BF),
            pltpu.VMEM((1024, 128), I32),
            pltpu.VMEM((4, 2, 16, 16, 512), BF),
            pltpu.VMEM((4, 16, 16, 512), BF),
            pltpu.VMEM((HALF, 16, 256), BF),
            pltpu.VMEM((HALF, 8, 128), I32),
            pltpu.VMEM((4, 144, 256), BF),
            pltpu.VMEM((4, 128, 256), BF),
            pltpu.VMEM((HALF, 144, 128), F32),
            pltpu.VMEM((8, 1024, 128), F32),
            pltpu.VMEM((2, 1024, 1024), BF),
            pltpu.VMEM((2, 512, 1024), BF),
            pltpu.VMEM((512, 1024), BF),
            dma, dma((4,)), dma, dma, dma((2,)), dma, dma, dma((4,)), dma((4,)),
            dma((4,)), dma((4,)), dma,
        ],
        compiler_params=pltpu.CompilerParams(
            collective_id=0, has_side_effects=True, vmem_limit_bytes=56 << 20
        ),
    )(offset, mid, count, traces, table)


def mix_kernel(own_ref, other_ref, op_ref, out_ref):
    core = lax.axis_index("kx")
    z = jnp.concatenate([own_ref[...], other_ref[...]], axis=1)
    res = nt(z, op_ref[0])
    out_ref[0, 0] = res[:, :128]
    out_ref[1, 0] = res[:, 128:]


def mix(own, other, op):
    return pl.pallas_call(
        mix_kernel,
        out_shape=jax.ShapeDtypeStruct((2, 8, 512, 128), F32),
        grid=(8,),
        in_specs=[
            pl.BlockSpec((512, 128), lambda f: (0, f)),
            pl.BlockSpec((512, 128), lambda f: (0, f)),
            pl.BlockSpec((1, 256, 256), lambda f: (f, 0, 0)),
        ],
        out_specs=pl.BlockSpec((2, 1, 512, 128), lambda f: (0, f, 0, 0)),
        compiler_params=pltpu.CompilerParams(vmem_limit_bytes=40 << 20),
    )(own, other, op)


def shards(traces, trace_offset, trace_midpoint, trace_count, operator, table):
    core = lax.axis_index("kx")
    own, other = spectra(
        trace_offset[None, :], trace_midpoint[None, :], trace_count[None, :], traces, table
    )
    re, im = operator[:, 0], operator[:, 1]
    op = jnp.stack([jnp.stack([re, -im], axis=2), jnp.stack([im, re], axis=2)], axis=1)
    op = op.reshape(8, 2, 128, 2, 2, HALF).transpose(0, 1, 2, 4, 3, 5)
    op = jnp.where(core == 0, op, op[:, :, :, ::-1]).reshape(8, 256, 256)
    return mix(own, other, op)


def solution(mesh):
    def run(traces, trace_offset, trace_midpoint, trace_count, operator):
        table = jnp.asarray(wave_tables(), BF)
        return jax.shard_map(
            shards,
            mesh=mesh,
            in_specs=(
                P(("off", "kx"), None),
                P(("off", "kx")),
                P(("off", "kx")),
                P(("off", "kx")),
                P("off", None, None, None),
                P(),
            ),
            out_specs=P(None, "off", "kx", None),
            check_vma=False,
        )(traces, trace_offset, trace_midpoint, trace_count, operator, table)

    return run
```

time: 129 us -> 75.5 us (0.59)
  blocking collectives: 53.9 us -> 0 us
  Pallas kernels: 52.4 us -> 67.3 us
  starting transfers between devices: 11.7 us -> 0 us
  other arithmetic: 3.58 us -> 0.52 us
    all_gather x1 -> x0, blocking collectives: 53.9 us -> none  [shards(): meta = lax.all_gather(coded, ('off', 'kx'))]
    pallas_call x2 -> x1, Pallas kernels: 47.5 us -> 62.4 us  [spectra(): pl.pallas_call(main_kernel, out_shape=(half, half), in_specs=[VMEM_SPEC]...]
    all_to_all x1 -> x0, starting transfers between devices: 11.5 us -> none  [shards(): lax.all_to_all(outgoing, ('off', 'kx'), split_axis=0, concat_axis=0, tile...]
    select_n x2 -> x1, other arithmetic: 1.69 us -> 0.35 us  [shards(): op = jnp.where(core == 0, op, op[:, :, :, ::-1]).reshape(8, 256, 256)]
    unnamed x9 -> x6, local copies, waits for them, and re-layouts: 1.69 us -> 2.8 us
    reshape x3 -> x2, local copies, waits for them, and re-layouts: 3.71 us -> 2.88 us  [shards(): op = jnp.where(core == 0, op, op[:, :, :, ::-1]).reshape(8, 256, 256)]
  transfers between devices with their start and end apart: 2 -> 0, of which waited for: 0 -> 0; matrix products, arithmetic and copies ran while one was open for 4% -> 0% of each run, Pallas kernels for 0% -> 0%
where the time goes in v2:
time: 75.5 us; the launch traced here: 75.3 us
  Pallas kernels  67.3 us (89%)
  local copies, waits for them, and re-layouts  6.75 us (9%)
    pallas_call x1, Pallas kernels, spectra(): pl.pallas_call(main_kernel, out_shape=(half, half), in_specs=[VMEM_SPEC]...  62.4 us
    pallas_call x1, Pallas kernels, mix(): pl.pallas_call(mix_kernel, out_shape=jax.ShapeDtypeStruct((2, 8, 512, 128...  4.88 us
    reshape x2, local copies, waits for them, and re-layouts, shards(): op = jnp.where(core == 0, op, op[:, :, :, ::-1]).reshape(8, 256, 256)  2.88 us
    unnamed x6, local copies, waits for them, and re-layouts  2.8 us

profile of v2, /device:TPU:1, one launch (start us, length us, event | category | flops | bytes accessed | tf_op | source)
XLA Modules:
  0.0 75.3 jit_solution(10207271103134109371)
XLA Ops:
  0.7 1.1 %fusion = (bf16[8,1,128,128]{3,2,1,0:T(8,128)(2,1)S(1)}, bf16[8,1,128,128]{3,2,1,0:T(8,128)(2,1)S(1)}) fusion(bf16[8,2,128,128]{3,2,1,0:T(8,128)(2,1)} %param.10), kind=kLoop, calls=%fused_computation.2 | loop fusion | bytes 1048576 | tf_op jit(solution)/shard_map/slice | solution.py:397
  1.7 0.2 copy.18
  1.9 0.1 neg.11
  2.0 0.2 copy.17
  2.2 0.1 maximum_bitcast_fusion
  2.3 0.4 reverse_select_fusion
  2.6 1.5 %copy.15 = bf16[8,2,128,2,2,64]{5,4,3,2,1,0:T(2,128)(2,1)S(1)} copy(bf16[8,2,128,2,2,64]{2,5,3,0,4,1:T(8,128)(2,1)S(1)} %reverse_select_fusion) | data formatting | bytes 2097152 | tf_op jit(solution)/shard_map/reshape | solution.py:400
  4.2 1.4 %reshape.27.op_ref = bf16[8,256,256]{2,1,0:T(8,128)(2,1)S(1)} reshape(bf16[8,2,128,2,2,64]{5,4,3,2,1,0:T(2,128)(2,1)S(1)} %copy.15) | data formatting | bytes 2097152 | tf_op jit(solution)/shard_map/reshape | solution.py:400
  5.5 62.4 %shard_map.64 = (bf16[512,1024]{1,0:T(8,128)(2,1)}, bf16[512,1024]{1,0:T(8,128)(2,1)}) custom-call(s32[1,512]{1,0:T(1,128)} %bitcast.11, s32[1,512]{1,0:T(1,128)} %bitcast.12, s32[1,1]{1,0:T(1,128)} %bitcast.7.cnt_ref, bf16[512,1024]{1,0:T(8,128)(2,1)} %traces_ref.1, bf16[2,512,1024]{2,1,0:T(8,128)(2,1)} %constant.8.clone.table_hbm), custom_call_target="tpu_custom_call" | custom-call | tf_op jit(solution)/shard_map/pallas_call | solution.py:339
  67.9 0.0 copy-start
  67.9 1.2 %copy-done = bf16[512,1024]{1,0:T(8,128)(2,1)S(1)} copy-done((bf16[512,1024]{1,0:T(8,128)(2,1)S(1)}, bf16[512,1024]{1,0:T(8,128)(2,1)}, u32[]{:S(2)}) %copy-start) | copy-done | bytes 1048600
  69.1 0.0 copy-start.1
  69.1 1.2 %copy-done.1 = bf16[512,1024]{1,0:T(8,128)(2,1)S(1)} copy-done((bf16[512,1024]{1,0:T(8,128)(2,1)S(1)}, bf16[512,1024]{1,0:T(8,128)(2,1)}, u32[]{:S(2)}) %copy-start.1) | copy-done | bytes 1048600
  70.4 4.9 %shard_map.65 = f32[2,8,512,128]{3,2,1,0:T(8,128)} custom-call(bf16[512,1024]{1,0:T(8,128)(2,1)S(1)} %copy-done, bf16[512,1024]{1,0:T(8,128)(2,1)S(1)} %copy-done.1, bf16[8,256,256]{2,1,0:T(8,128)(2,1)S(1)} %reshape.27.op_ref), custom_call_target="tpu_custom_call" | custom-call | tf_op jit(solution)/shard_map/pallas_call | solution.py:378
Async XLA Ops:
  67.9 1.2 %copy-start = (bf16[512,1024]{1,0:T(8,128)(2,1)S(1)}, bf16[512,1024]{1,0:T(8,128)(2,1)}, u32[]{:S(2)}) copy-start(bf16[512,1024]{1,0:T(8,128)(2,1)} %get-tuple-element.7.own_ref) | copy-start | bytes 3145732
  69.1 1.2 %copy-start.1 = (bf16[512,1024]{1,0:T(8,128)(2,1)S(1)}, bf16[512,1024]{1,0:T(8,128)(2,1)}, u32[]{:S(2)}) copy-start(bf16[512,1024]{1,0:T(8,128)(2,1)} %get-tuple-element.8.other_ref) | copy-start | bytes 3145732

commit v3 on v2

--- a/solution.py
+++ b/solution.py
@@ -12,13 +12,16 @@
 ROWS = 512
 CHIPS = 64
 HALF = 64
+UNROLL = 16
+AHEAD = 4
+FREQS = 4
 BF = jnp.bfloat16
 F32 = jnp.float32
 I32 = jnp.int32
 MESH = pl.DeviceIdType.MESH
 
 VMEM_SPEC = pl.BlockSpec(memory_space=pltpu.VMEM)
-ANY_SPEC = pl.BlockSpec(memory_space=pl.ANY)
+HBM_SPEC = pl.BlockSpec(memory_space=pltpu.HBM)
 
 
 def nt(a, b):
@@ -109,10 +112,10 @@
 
 
 def main_kernel(
-    off_ref, mid_ref, cnt_ref, traces_ref, table_hbm, own_ref, other_ref,
-    blocks, meta_out, got, meta, ex, dx, y_ref, mm, left, hot, acc, s32, s16, table, give,
+    off_hbm, mid_hbm, cnt_hbm, traces_hbm, table_hbm, own_ref, other_ref,
+    off_ref, mid_ref, cnt_ref, traces_ref, blocks, meta_out, got, meta, ex, dx, y_ref, mm, acc, s32, s16, table, give, own_part,
     send_sem, recv_sem, msend_sem, mrecv_sem, local_sem, mx_send, mx_recv, dx_send, dx_recv,
-    sp_send, sp_recv, table_sem,
+    sp_send, sp_recv, load_sem, put_sem,
 ):
     off, core = lax.axis_index("off"), lax.axis_index("kx")
     xy = off % 16
@@ -120,6 +123,14 @@
     me = (total % 4) * 16 + xy
     mate = (off, 1 - core)
 
+    loads = [
+        pltpu.make_async_copy(src, dst, load_sem.at[n])
+        for n, (src, dst) in enumerate(
+            [(off_hbm, off_ref), (mid_hbm, mid_ref), (cnt_hbm, cnt_ref), (traces_hbm, traces_ref), (table_hbm, table)]
+        )
+    ]
+    for load in loads[:4]:
+        load.start()
     bar = pltpu.get_barrier_semaphore()
 
     def greet(n, _):
@@ -129,8 +140,9 @@
 
     lax.fori_loop(1, CHIPS, greet, 0)
     pl.semaphore_signal(bar, inc=1, device_id=mate, device_id_type=MESH)
-    load_table = pltpu.make_async_copy(table_hbm, table, table_sem)
-    load_table.start()
+    for load in loads[:4]:
+        load.wait()
+    loads[4].start()
 
     sort_rows(xy, off_ref, mid_ref, cnt_ref, traces_ref, blocks, meta_out)
 
@@ -159,7 +171,7 @@
         return 0
 
     lax.fori_loop(1, CHIPS, send_meta, 0)
-    lax.fori_loop(1, CHIPS, send_block, 0)
+    lax.fori_loop(1, AHEAD * 16, send_block, 0)
 
     def clear(w, _):
         acc[w] = jnp.zeros((144, 128), F32)
@@ -188,9 +200,13 @@
 
     lax.fori_loop(0, 4, meta_by_owner, 0)
 
-    def one_round(r, _):
-        kind = (total + 4 - r) % 4
-        base = kind * 16
+    def exchange(r):
+        return pltpu.make_async_remote_copy(
+            ex.at[r, 1 - core], dx.at[r], dx_send.at[r], dx_recv.at[r], device_id=mate, device_id_type=MESH
+        )
+
+    def take_in(r):
+        base = (total + 4 - r) % 4 * 16
 
         def arrived(n):
             part = got.at[pl.ds(0, n)]
@@ -206,6 +222,10 @@
         @pl.when(r > 0)
         def _():
             arrived(16)
+
+        @pl.when(r < 4 - AHEAD)
+        def _():
+            lax.fori_loop((r + AHEAD) * 16, (r + AHEAD + 1) * 16, send_block, 0)
 
         def expand(s, _):
             n = base + s
@@ -223,11 +243,12 @@
                 ex[r, c // 4, s, :, (c % 4) * 128 : (c % 4) * 128 + 128] = out.astype(BF)
             return 0
 
-        lax.fori_loop(0, 16, expand, 0, unroll=4)
-        swap = pltpu.make_async_remote_copy(
-            ex.at[r, 1 - core], dx.at[r], dx_send.at[r], dx_recv.at[r], device_id=mate, device_id_type=MESH
-        )
-        swap.start()
+        lax.fori_loop(0, 16, expand, 0, unroll=8)
+        exchange(r).start()
+
+    def one_round(r, last):
+        kind = (total + 4 - r) % 4
+        exchange(r).wait()
 
         def by_owner(which, col):
             lanes = pl.ds(pl.multiple_of(col * 128, 128), 128)
@@ -238,64 +259,61 @@
             for w, part in enumerate(regroup(parts, group16)):
                 y_ref[col * 16 + w, :, which * 128 : which * 128 + 128] = part
 
-        def own_cols(col, _):
+        def both_cols(col, _):
             by_owner(0, col)
-            return 0
-
-        def mate_cols(col, _):
             by_owner(1, col)
             return 0
 
-        lax.fori_loop(0, 4, own_cols, 0)
-        swap.wait()
-        lax.fori_loop(0, 4, mate_cols, 0)
-
-        def four_owners(w4, _):
+        lax.fori_loop(0, 4, both_cols, 0)
+
+        def some_owners(g, _):
             row_id = lax.broadcasted_iota(I32, (128, 128), 0).astype(F32).astype(BF)
             one, zero = jnp.ones((), BF), jnp.zeros((), BF)
-            for u in range(4):
-                w = w4 * 4 + u
+            for u in range(UNROLL):
+                w = g * UNROLL + u
+                left, hot = [], []
                 for which in range(2):
-                    lanes = slice(which * 128, which * 128 + 128)
                     code = mm[w, pl.ds(which * 4 + kind, 1), :]
                     combo = (code // 131072).astype(F32)
                     low = ((code // 1024) % 128).astype(F32)
                     combo = jnp.broadcast_to(combo, (16, 128)).astype(BF)
                     low = jnp.broadcast_to(low, (128, 128)).astype(BF)
-                    data = y_ref[w, :, lanes]
-                    for q in range(8):
-                        left[u, q * 16 : q * 16 + 16, lanes] = jnp.where(
-                            combo == jnp.asarray(q + 1, BF), data, zero
-                        )
-                    left[u, 128:144, lanes] = jnp.where(combo == row_id[:16] + one, one, zero)
-                    hot[u, :, lanes] = jnp.where(low == row_id, one, zero)
-                acc[w] += nt(left[u], hot[u])
+                    data = y_ref[w, :, which * 128 : which * 128 + 128]
+                    rows = [jnp.where(combo == jnp.asarray(q + 1, BF), data, zero) for q in range(8)]
+                    rows.append(jnp.where(combo == row_id[:16] + one, one, zero))
+                    left.append(jnp.concatenate(rows, axis=0))
+                    hot.append(jnp.where(low == row_id, one, zero))
+                cells = nt(jnp.concatenate(left, axis=1), jnp.concatenate(hot, axis=1))
+                if not last:
+                    acc[w] += cells
+                    continue
+                cells = acc[w] + cells
+                scale = 1.0 / jnp.maximum(cells[128:136], 1.0)
+                for q in range(8):
+                    o2, par, b8 = q // 4, (q // 2) % 2, q % 2
+                    mean = cells[q * 16 : q * 16 + 16] * scale[q : q + 1]
+                    cells_of = s32.at[par * 4 + (u % 2) * 2 + b8]
+                    row = g * UNROLL + u // 2 * 2 + o2
+                    cells_of[pl.ds(row, 8, stride=128), :] = mean[:8]
+                    cells_of[pl.ds(64 + row, 8, stride=128), :] = mean[8:]
             return 0
 
-        lax.fori_loop(0, HALF // 4, four_owners, 0)
-        return 0
-
-    lax.fori_loop(0, 4, one_round, 0)
+        lax.fori_loop(0, HALF // UNROLL, some_owners, 0)
+
+    def round_of(r, _):
+        take_in(r)
+        one_round(r - 1, False)
+        return 0
+
+    take_in(jnp.int32(0))
+    lax.fori_loop(1, 4, round_of, 0)
+    one_round(jnp.int32(3), True)
     sent = blocks.at[pl.ds(0, 63)]
     pltpu.make_async_remote_copy(
         sent, sent, send_sem, recv_sem.at[0], device_id=mate, device_id_type=MESH
     ).wait_send()
 
-    def means(w, _):
-        pair, h = w // 2, w % 2
-        fold = jnp.maximum(acc[w, 128:136], 1.0)
-        for q in range(8):
-            o2, par, b8 = q // 4, (q // 2) % 2, q % 2
-            mean = acc[w, q * 16 : q * 16 + 16] / fold[q : q + 1]
-            cells_of = s32.at[par * 4 + h * 2 + b8]
-            row = pair * 2 + o2
-            cells_of[pl.ds(row, 8, stride=128), :] = mean[:8]
-            cells_of[pl.ds(64 + row, 8, stride=128), :] = mean[8:]
-        return 0
-
-    lax.fori_loop(0, HALF, means, 0)
-
-    load_table.wait()
+    loads[4].wait()
     sign = (1 - 2 * core).astype(F32)
 
     def handing(j):
@@ -304,6 +322,10 @@
             give.at[:, lanes], other_ref.at[:, lanes], sp_send.at[j], sp_recv.at[j],
             device_id=mate, device_id_type=MESH,
         )
+
+    def putting(j):
+        lanes = pl.ds(pl.multiple_of(j * 256, 256), 256)
+        return pltpu.make_async_copy(own_part.at[:, lanes], own_ref.at[:, lanes], put_sem.at[j])
 
     def transform(j, _):
         for f in range(2):
@@ -319,7 +341,8 @@
         r0 = pl.multiple_of(j * 256, 256)
         even = nt(table[0], s16[0, pl.ds(r0, 256), :])
         odd = nt(table[1], s16[1, pl.ds(r0, 256), :]) * sign
-        own_ref[:, pl.ds(r0, 256)] = (even + odd).astype(BF)
+        own_part[:, pl.ds(r0, 256)] = (even + odd).astype(BF)
+        putting(j).start()
         give[:, pl.ds(r0, 256)] = (even - odd).astype(BF)
         handing(j).start()
         return 0
@@ -327,6 +350,7 @@
     lax.fori_loop(0, 4, transform, 0)
 
     def handed(j, _):
+        putting(j).wait()
         handing(j).wait()
         return 0
 
@@ -339,9 +363,13 @@
     return pl.pallas_call(
         main_kernel,
         out_shape=(half, half),
-        in_specs=[VMEM_SPEC] * 4 + [ANY_SPEC],
-        out_specs=(VMEM_SPEC, VMEM_SPEC),
+        in_specs=[HBM_SPEC] * 5,
+        out_specs=(HBM_SPEC, HBM_SPEC),
         scratch_shapes=[
+            pltpu.VMEM((1, ROWS), I32),
+            pltpu.VMEM((1, ROWS), I32),
+            pltpu.VMEM((1, 1), I32),
+            pltpu.VMEM((ROWS, 2 * NF), BF),
             pltpu.VMEM((CHIPS, 16, ROWS), BF),
             pltpu.VMEM((8, 128), I32),
             pltpu.VMEM((CHIPS, 16, ROWS), BF),
@@ -350,55 +378,64 @@
             pltpu.VMEM((4, 16, 16, 512), BF),
             pltpu.VMEM((HALF, 16, 256), BF),
             pltpu.VMEM((HALF, 8, 128), I32),
-            pltpu.VMEM((4, 144, 256), BF),
-            pltpu.VMEM((4, 128, 256), BF),
             pltpu.VMEM((HALF, 144, 128), F32),
             pltpu.VMEM((8, 1024, 128), F32),
             pltpu.VMEM((2, 1024, 1024), BF),
             pltpu.VMEM((2, 512, 1024), BF),
             pltpu.VMEM((512, 1024), BF),
+            pltpu.VMEM((512, 1024), BF),
             dma, dma((4,)), dma, dma, dma((2,)), dma, dma, dma((4,)), dma((4,)),
-            dma((4,)), dma((4,)), dma,
+            dma((4,)), dma((4,)), dma((5,)), dma((4,)),
         ],
         compiler_params=pltpu.CompilerParams(
-            collective_id=0, has_side_effects=True, vmem_limit_bytes=56 << 20
+            collective_id=0, has_side_effects=True, vmem_limit_bytes=62 << 20
         ),
     )(offset, mid, count, traces, table)
 
 
 def mix_kernel(own_ref, other_ref, op_ref, out_ref):
     core = lax.axis_index("kx")
-    z = jnp.concatenate([own_ref[...], other_ref[...]], axis=1)
-    res = nt(z, op_ref[0])
-    out_ref[0, 0] = res[:, :128]
-    out_ref[1, 0] = res[:, 128:]
+    lower = lax.broadcasted_iota(I32, (128, 128), 1) < HALF
+    for f in range(FREQS):
+        re = op_ref[f, 0]
+        im = op_ref[f, 1]
+        re_turned, im_turned = pltpu.roll(re, HALF, axis=1), pltpu.roll(im, HALF, axis=1)
+        first = core == 0
+        re, re_turned = jnp.where(first, re, re_turned), jnp.where(first, re_turned, re)
+        im, im_turned = jnp.where(first, im, im_turned), jnp.where(first, im_turned, im)
+        by_own = jnp.concatenate(
+            [jnp.where(lower, re, -im_turned), jnp.where(lower, im, re_turned)], axis=0
+        )
+        by_other = jnp.concatenate(
+            [jnp.where(lower, re_turned, -im), jnp.where(lower, im_turned, re)], axis=0
+        )
+        lanes = slice(f * 128, f * 128 + 128)
+        z = jnp.concatenate([own_ref[:, lanes], other_ref[:, lanes]], axis=1)
+        res = nt(z, jnp.concatenate([by_own, by_other], axis=1))
+        out_ref[0, f] = res[:, :128]
+        out_ref[1, f] = res[:, 128:]
 
 
 def mix(own, other, op):
     return pl.pallas_call(
         mix_kernel,
         out_shape=jax.ShapeDtypeStruct((2, 8, 512, 128), F32),
-        grid=(8,),
+        grid=(8 // FREQS,),
         in_specs=[
-            pl.BlockSpec((512, 128), lambda f: (0, f)),
-            pl.BlockSpec((512, 128), lambda f: (0, f)),
-            pl.BlockSpec((1, 256, 256), lambda f: (f, 0, 0)),
+            pl.BlockSpec((512, FREQS * 128), lambda f: (0, f)),
+            pl.BlockSpec((512, FREQS * 128), lambda f: (0, f)),
+            pl.BlockSpec((FREQS, 2, 128, 128), lambda f: (f, 0, 0, 0)),
         ],
-        out_specs=pl.BlockSpec((2, 1, 512, 128), lambda f: (0, f, 0, 0)),
-        compiler_params=pltpu.CompilerParams(vmem_limit_bytes=40 << 20),
+        out_specs=pl.BlockSpec((2, FREQS, 512, 128), lambda f: (0, f, 0, 0)),
+        compiler_params=pltpu.CompilerParams(vmem_limit_bytes=62 << 20),
     )(own, other, op)
 
 
 def shards(traces, trace_offset, trace_midpoint, trace_count, operator, table):
-    core = lax.axis_index("kx")
     own, other = spectra(
         trace_offset[None, :], trace_midpoint[None, :], trace_count[None, :], traces, table
     )
-    re, im = operator[:, 0], operator[:, 1]
-    op = jnp.stack([jnp.stack([re, -im], axis=2), jnp.stack([im, re], axis=2)], axis=1)
-    op = op.reshape(8, 2, 128, 2, 2, HALF).transpose(0, 1, 2, 4, 3, 5)
-    op = jnp.where(core == 0, op, op[:, :, :, ::-1]).reshape(8, 256, 256)
-    return mix(own, other, op)
+    return mix(own, other, operator)
 
 
 def solution(mesh):

time: 75.5 us -> 51.3 us (0.68)
  Pallas kernels: 67.3 us -> 50.5 us
  local copies, waits for them, and re-layouts: 6.75 us -> 0 us
    pallas_call x1, Pallas kernels: 62.4 us -> 46.7 us  [spectra(): pl.pallas_call(main_kernel, out_shape=(half, half), in_specs=[HBM_SPEC] *...]
    reshape x2 -> x0, local copies, waits for them, and re-layouts: 2.88 us -> none  [shards(): op = jnp.where(core == 0, op, op[:, :, :, ::-1]).reshape(8, 256, 256)]
    unnamed x6 -> x0, local copies, waits for them, and re-layouts: 2.8 us -> none
    slice x1 -> x0, local copies, waits for them, and re-layouts: 1.07 us -> none  [shards(): re, im = (operator[:, 0], operator[:, 1])]
    pallas_call x1, Pallas kernels: 4.88 us -> 3.86 us  [mix(): pl.pallas_call(mix_kernel, out_shape=jax.ShapeDtypeStruct((2, 8, 512, 128...]
where the time goes in v3:
time: 51.3 us; the launch traced here: 51.2 us
  Pallas kernels  50.5 us (98%)
  between operations  0.66 us (1%)
    pallas_call x1, Pallas kernels, spectra(): pl.pallas_call(main_kernel, out_shape=(half, half), in_specs=[HBM_SPEC] *...  46.7 us
    pallas_call x1, Pallas kernels, mix(): pl.pallas_call(mix_kernel, out_shape=jax.ShapeDtypeStruct((2, 8, 512, 128...  3.86 us

profile of v3, /device:TPU:1, one launch (start us, length us, event | category | flops | bytes accessed | tf_op | source)
XLA Modules:
  0.0 51.2 jit_solution(18045458228650739439)
XLA Ops:
  0.7 46.7 %shard_map.64 = (bf16[512,1024]{1,0:T(8,128)(2,1)}, bf16[512,1024]{1,0:T(8,128)(2,1)}) custom-call(s32[1,512]{1,0:T(1,128)} %bitcast.4, s32[1,512]{1,0:T(1,128)} %bitcast.5, s32[1,1]{1,0:T(1,128)} %bitcast.3.cnt_hbm, bf16[512,1024]{1,0:T(8,128)(2,1)} %traces_hbm.1, bf16[2,512,1024]{2,1,0:T(8,128)(2,1)} %constant.2.clone.table_hbm), custom_call_target="tpu_custom_call" | custom-call | tf_op jit(solution)/shard_map/pallas_call | solution.py:363
  47.3 3.9 %shard_map.65 = f32[2,8,512,128]{3,2,1,0:T(8,128)} custom-call(bf16[512,1024]{1,0:T(8,128)(2,1)} %get-tuple-element.7.own_ref, bf16[512,1024]{1,0:T(8,128)(2,1)} %get-tuple-element.8.other_ref, bf16[8,2,128,128]{3,2,1,0:T(8,128)(2,1)} %op_ref.1), custom_call_target="tpu_custom_call" | custom-call | tf_op jit(solution)/shard_map/pallas_call | solution.py:420

commit v4 on v3

--- a/solution.py
+++ b/solution.py
@@ -12,7 +12,9 @@
 ROWS = 512
 CHIPS = 64
 HALF = 64
-UNROLL = 16
+UNROLL = 32
+WIDTH = 256
+DFT_UNROLL = 2
 AHEAD = 4
 FREQS = 4
 BF = jnp.bfloat16
@@ -29,12 +31,10 @@
 
 
 def wave_tables():
-    k = np.arange(512)
+    k = np.arange(256)
     tables = []
-    for par in range(2):
-        m = np.concatenate(
-            [h * 512 + b * 256 + np.arange(128) * 2 + par for h in range(2) for b in range(2)]
-        )
+    for residue in range(4):
+        m = np.concatenate([h * 512 + np.arange(128) * 4 + residue for h in range(2)])
         angle = (k[:, None] * m[None, :]) % NM * (2.0 * np.pi / NM)
         tables.append(np.concatenate([np.cos(angle), np.sin(angle)], axis=1))
     return np.stack(tables).astype(np.float32)
@@ -68,8 +68,8 @@
     slot = (owner // 16) * 128 + ((owner % 16 + xy) % 16) * CAP + rank
     slot = jnp.where(live, slot, -1)
 
-    combo = (offset % 2) * 4 + (mid % 2) * 2 + (mid // 256) % 2 + 1
-    low = (mid % 256) // 2
+    combo = (offset % 2) * 4 + mid % 4 + 1
+    low = (mid % 512) // 4
     fields = jnp.concatenate(
         [position % 128, low, combo, jnp.zeros((13, ROWS), I32)], axis=0
     ).astype(F32).astype(BF)
@@ -290,12 +290,12 @@
                 cells = acc[w] + cells
                 scale = 1.0 / jnp.maximum(cells[128:136], 1.0)
                 for q in range(8):
-                    o2, par, b8 = q // 4, (q // 2) % 2, q % 2
+                    o2, residue = q // 4, q % 4
                     mean = cells[q * 16 : q * 16 + 16] * scale[q : q + 1]
-                    cells_of = s32.at[par * 4 + (u % 2) * 2 + b8]
+                    cells_of = s32.at[residue * 2 + u % 2]
                     row = g * UNROLL + u // 2 * 2 + o2
-                    cells_of[pl.ds(row, 8, stride=128), :] = mean[:8]
-                    cells_of[pl.ds(64 + row, 8, stride=128), :] = mean[8:]
+                    cells_of[pl.ds(row, 8, stride=136), :] = mean[:8]
+                    cells_of[pl.ds(64 + row, 8, stride=136), :] = mean[8:]
             return 0
 
         lax.fori_loop(0, HALF // UNROLL, some_owners, 0)
@@ -317,44 +317,54 @@
     sign = (1 - 2 * core).astype(F32)
 
     def handing(j):
-        lanes = pl.ds(pl.multiple_of(j * 256, 256), 256)
+        lanes = pl.ds(pl.multiple_of(j * WIDTH, WIDTH), WIDTH)
         return pltpu.make_async_remote_copy(
             give.at[:, lanes], other_ref.at[:, lanes], sp_send.at[j], sp_recv.at[j],
             device_id=mate, device_id_type=MESH,
         )
 
     def putting(j):
-        lanes = pl.ds(pl.multiple_of(j * 256, 256), 256)
+        lanes = pl.ds(pl.multiple_of(j * WIDTH, WIDTH), WIDTH)
         return pltpu.make_async_copy(own_part.at[:, lanes], own_ref.at[:, lanes], put_sem.at[j])
 
     def transform(j, _):
-        for f in range(2):
-            r0 = pl.multiple_of(j * 256 + f * 128, 128)
-            for lb in range(8):
-                par, lane0 = lb // 4, (lb % 4) * 128
-                re = s32[lb, pl.ds(r0, 64), :].astype(BF)
-                im = s32[lb, pl.ds(r0 + 64, 64), :].astype(BF)
-                s16[par, pl.ds(r0, 64), lane0 : lane0 + 128] = re
-                s16[par, pl.ds(r0 + 64, 64), lane0 : lane0 + 128] = im
-                s16[par, pl.ds(r0, 64), 512 + lane0 : 640 + lane0] = im
-                s16[par, pl.ds(r0 + 64, 64), 512 + lane0 : 640 + lane0] = -re
-        r0 = pl.multiple_of(j * 256, 256)
-        even = nt(table[0], s16[0, pl.ds(r0, 256), :])
-        odd = nt(table[1], s16[1, pl.ds(r0, 256), :]) * sign
-        own_part[:, pl.ds(r0, 256)] = (even + odd).astype(BF)
+        r0 = pl.multiple_of(j * WIDTH, WIDTH)
+        spec = []
+        for n in range(4):
+            xs = []
+            for f in range(WIDTH // 128):
+                q0 = pl.multiple_of((j * (WIDTH // 128) + f) * 136, 8)
+                re = [s32[2 * n + h, pl.ds(q0, 64), :].astype(BF) for h in range(2)]
+                im = [s32[2 * n + h, pl.ds(q0 + 64, 64), :].astype(BF) for h in range(2)]
+                xs.append(jnp.concatenate(re + im, axis=1))
+                xs.append(jnp.concatenate(im + [-re[0], -re[1]], axis=1))
+            spec.append(nt(table[n], jnp.concatenate(xs, axis=0)))
+        f0, f1, f2, f3 = spec
+        real = lax.broadcasted_iota(I32, (256, 128), 1) < HALF
+        odd = (f1 + f3) * sign
+        diff = (f1 - f3) * sign
+        turned = []
+        for f in range(WIDTH // 128):
+            part = pltpu.roll(diff[:, f * 128 : f * 128 + 128], HALF, axis=1)
+            turned.append(jnp.where(real, part, -part))
+        turned = jnp.concatenate(turned, axis=1) if len(turned) > 1 else turned[0]
+        lanes = pl.ds(r0, WIDTH)
+        give[:256, lanes] = (f0 + f2 - odd).astype(BF)
+        give[256:, lanes] = (f0 - f2 - turned).astype(BF)
+        handing(j).start()
+        own_part[:256, lanes] = (f0 + f2 + odd).astype(BF)
+        own_part[256:, lanes] = (f0 - f2 + turned).astype(BF)
         putting(j).start()
-        give[:, pl.ds(r0, 256)] = (even - odd).astype(BF)
-        handing(j).start()
-        return 0
-
-    lax.fori_loop(0, 4, transform, 0)
+        return 0
+
+    lax.fori_loop(0, 1024 // WIDTH, transform, 0, unroll=DFT_UNROLL)
 
     def handed(j, _):
         putting(j).wait()
         handing(j).wait()
         return 0
 
-    lax.fori_loop(0, 4, handed, 0)
+    lax.fori_loop(0, 1024 // WIDTH, handed, 0)
 
 
 def spectra(offset, mid, count, traces, table):
@@ -379,13 +389,13 @@
             pltpu.VMEM((HALF, 16, 256), BF),
             pltpu.VMEM((HALF, 8, 128), I32),
             pltpu.VMEM((HALF, 144, 128), F32),
-            pltpu.VMEM((8, 1024, 128), F32),
-            pltpu.VMEM((2, 1024, 1024), BF),
-            pltpu.VMEM((2, 512, 1024), BF),
+            pltpu.VMEM((8, 1088, 128), F32),
+            pltpu.VMEM((4, 1024, 512), BF),
+            pltpu.VMEM((4, 256, 512), BF),
             pltpu.VMEM((512, 1024), BF),
             pltpu.VMEM((512, 1024), BF),
             dma, dma((4,)), dma, dma, dma((2,)), dma, dma, dma((4,)), dma((4,)),
-            dma((4,)), dma((4,)), dma((5,)), dma((4,)),
+            dma((8,)), dma((8,)), dma((5,)), dma((8,)),
         ],
         compiler_params=pltpu.CompilerParams(
             collective_id=0, has_side_effects=True, vmem_limit_bytes=62 << 20

time: 51.3 us -> 46.1 us (0.90)
  Pallas kernels: 50.5 us -> 45.3 us
    pallas_call x1, Pallas kernels: 46.7 us -> 41.4 us  [spectra(): pl.pallas_call(main_kernel, out_shape=(half, half), in_specs=[HBM_SPEC] *...]
where the time goes in v4:
time: 46.1 us; the launch traced here: 45.9 us
  Pallas kernels  45.3 us (98%)
  between operations  0.66 us (1%)
    pallas_call x1, Pallas kernels, spectra(): pl.pallas_call(main_kernel, out_shape=(half, half), in_specs=[HBM_SPEC] *...  41.4 us
    pallas_call x1, Pallas kernels, mix(): pl.pallas_call(mix_kernel, out_shape=jax.ShapeDtypeStruct((2, 8, 512, 128...  3.86 us

profile of v4, /device:TPU:1, one launch (start us, length us, event | category | flops | bytes accessed | tf_op | source)
XLA Modules:
  0.0 45.9 jit_solution(6705316848025139756)
XLA Ops:
  0.7 41.4 %shard_map.64 = (bf16[512,1024]{1,0:T(8,128)(2,1)}, bf16[512,1024]{1,0:T(8,128)(2,1)}) custom-call(s32[1,512]{1,0:T(1,128)} %bitcast.4, s32[1,512]{1,0:T(1,128)} %bitcast.5, s32[1,1]{1,0:T(1,128)} %bitcast.3.cnt_hbm, bf16[512,1024]{1,0:T(8,128)(2,1)} %traces_hbm.1, bf16[4,256,512]{2,1,0:T(8,128)(2,1)} %constant.2.clone.table_hbm), custom_call_target="tpu_custom_call" | custom-call | tf_op jit(solution)/shard_map/pallas_call | solution.py:373
  42.1 3.9 %shard_map.65 = f32[2,8,512,128]{3,2,1,0:T(8,128)} custom-call(bf16[512,1024]{1,0:T(8,128)(2,1)} %get-tuple-element.7.own_ref, bf16[512,1024]{1,0:T(8,128)(2,1)} %get-tuple-element.8.other_ref, bf16[8,2,128,128]{3,2,1,0:T(8,128)(2,1)} %op_ref.1), custom_call_target="tpu_custom_call" | custom-call | tf_op jit(solution)/shard_map/pallas_call | solution.py:430

commit v5 on v4

--- a/solution.py
+++ b/solution.py
@@ -14,7 +14,7 @@
 HALF = 64
 UNROLL = 32
 WIDTH = 256
-DFT_UNROLL = 2
+DFT_UNROLL = 4
 AHEAD = 4
 FREQS = 4
 BF = jnp.bfloat16
@@ -41,10 +41,9 @@
 
 
 def shifted(off, r, i):
-    z, x, y = off // 16, (off // 4) % 4, off % 4
-    dx, dy = i // 4, i % 4
-    dz = (r + 8 - dx - dy) % 4
-    return ((z + dz) % 4) * 16 + ((x + dx) % 4) * 4 + (y + dy) % 4
+    z, x, y = lax.div(off, 16), lax.rem(lax.div(off, 4), 4), lax.rem(off, 4)
+    dx, dy = lax.div(i, 4), lax.rem(i, 4)
+    return lax.rem(z + r + 8 - dx - dy, 4) * 16 + lax.rem(x + dx, 4) * 4 + lax.rem(y + dy, 4)
 
 
 def sort_rows(xy, off_ref, mid_ref, cnt_ref, traces_ref, blocks_ref, meta_ref):
@@ -134,7 +133,7 @@
     bar = pltpu.get_barrier_semaphore()
 
     def greet(n, _):
-        peer = shifted(off, n // 16, n % 16)
+        peer = shifted(off, lax.div(n, 16), lax.rem(n, 16))
         pl.semaphore_signal(bar, inc=1, device_id=(peer, core), device_id_type=MESH)
         return 0
 
@@ -156,16 +155,16 @@
     pl.semaphore_wait(bar, CHIPS)
 
     def send_meta(n, _):
-        peer = shifted(off, n // 16, n % 16)
+        peer = shifted(off, lax.div(n, 16), lax.rem(n, 16))
         pltpu.make_async_remote_copy(
             meta_out, meta_slot(0, me), msend_sem, mrecv_sem, device_id=(peer, core), device_id_type=MESH
         ).start()
         return 0
 
     def send_block(n, _):
-        peer = shifted(off, n // 16, n % 16)
+        peer = shifted(off, lax.div(n, 16), lax.rem(n, 16))
         pltpu.make_async_remote_copy(
-            blocks.at[peer], got.at[me], send_sem, recv_sem.at[n // 16],
+            blocks.at[peer], got.at[me], send_sem, recv_sem.at[lax.div(n, 16)],
             device_id=(peer, core), device_id_type=MESH,
         ).start()
         return 0
@@ -243,7 +242,7 @@
                 ex[r, c // 4, s, :, (c % 4) * 128 : (c % 4) * 128 + 128] = out.astype(BF)
             return 0
 
-        lax.fori_loop(0, 16, expand, 0, unroll=8)
+        lax.fori_loop(0, 16, expand, 0, unroll=16)
         exchange(r).start()
 
     def one_round(r, last):

time: 46.1 us -> 45.6 us (0.989)
  Pallas kernels: 45.3 us -> 44.8 us
where the time goes in v5:
time: 45.6 us; the launch traced here: 45.5 us
  Pallas kernels  44.8 us (98%)
  between operations  0.66 us (1%)
    pallas_call x1, Pallas kernels, spectra(): pl.pallas_call(main_kernel, out_shape=(half, half), in_specs=[HBM_SPEC] *...  41 us
    pallas_call x1, Pallas kernels, mix(): pl.pallas_call(mix_kernel, out_shape=jax.ShapeDtypeStruct((2, 8, 512, 128...  3.86 us

profile of v5, /device:TPU:1, one launch (start us, length us, event | category | flops | bytes accessed | tf_op | source)
XLA Modules:
  0.0 45.5 jit_solution(9304901388233119791)
XLA Ops:
  0.7 41.0 %shard_map.64 = (bf16[512,1024]{1,0:T(8,128)(2,1)}, bf16[512,1024]{1,0:T(8,128)(2,1)}) custom-call(s32[1,512]{1,0:T(1,128)} %bitcast.4, s32[1,512]{1,0:T(1,128)} %bitcast.5, s32[1,1]{1,0:T(1,128)} %bitcast.3.cnt_hbm, bf16[512,1024]{1,0:T(8,128)(2,1)} %traces_hbm.1, bf16[4,256,512]{2,1,0:T(8,128)(2,1)} %constant.2.clone.table_hbm), custom_call_target="tpu_custom_call" | custom-call | tf_op jit(solution)/shard_map/pallas_call | solution.py:372
  41.6 3.9 %shard_map.65 = f32[2,8,512,128]{3,2,1,0:T(8,128)} custom-call(bf16[512,1024]{1,0:T(8,128)(2,1)} %get-tuple-element.7.own_ref, bf16[512,1024]{1,0:T(8,128)(2,1)} %get-tuple-element.8.other_ref, bf16[8,2,128,128]{3,2,1,0:T(8,128)(2,1)} %op_ref.1), custom_call_target="tpu_custom_call" | custom-call | tf_op jit(solution)/shard_map/pallas_call | solution.py:429

commit v6 on v5

--- a/solution.py
+++ b/solution.py
@@ -46,7 +46,7 @@
     return lax.rem(z + r + 8 - dx - dy, 4) * 16 + lax.rem(x + dx, 4) * 4 + lax.rem(y + dy, 4)
 
 
-def sort_rows(xy, off_ref, mid_ref, cnt_ref, traces_ref, blocks_ref, meta_ref):
+def sort_rows(xy, off_ref, mid_ref, cnt_ref, traces_ref, blocks_ref, meta_ref, planned):
     offset, mid = off_ref[...], mid_ref[...]
     t = lax.broadcasted_iota(I32, (1, ROWS), 1)
     live = t < jnp.broadcast_to(cnt_ref[...], (1, ROWS))
@@ -85,6 +85,8 @@
 
     place = (lax.broadcasted_iota(I32, (ROWS, ROWS), 0) == position).astype(F32).astype(BF)
 
+    planned()
+
     def cut(j, _):
         lanes = pl.multiple_of(j * 128, 128)
         both = []
@@ -143,16 +145,10 @@
         load.wait()
     loads[4].start()
 
-    sort_rows(xy, off_ref, mid_ref, cnt_ref, traces_ref, blocks, meta_out)
-
     def meta_slot(which, n):
         return meta.at[pl.ds(pl.multiple_of(which * 512 + n * 8, 8), 8)]
 
-    keep = pltpu.make_async_copy(blocks.at[off], got.at[me], local_sem.at[0])
-    keep.start()
     keep_meta = pltpu.make_async_copy(meta_out, meta_slot(0, me), local_sem.at[1])
-    keep_meta.start()
-    pl.semaphore_wait(bar, CHIPS)
 
     def send_meta(n, _):
         peer = shifted(off, lax.div(n, 16), lax.rem(n, 16))
@@ -169,8 +165,15 @@
         ).start()
         return 0
 
-    lax.fori_loop(1, CHIPS, send_meta, 0)
-    lax.fori_loop(1, AHEAD * 16, send_block, 0)
+    def planned():
+        keep_meta.start()
+        pl.semaphore_wait(bar, CHIPS)
+        lax.fori_loop(1, CHIPS, send_meta, 0)
+
+    sort_rows(xy, off_ref, mid_ref, cnt_ref, traces_ref, blocks, meta_out, planned)
+    keep = pltpu.make_async_copy(blocks.at[off], got.at[me], local_sem.at[0])
+    keep.start()
+    lax.fori_loop(1, CHIPS, send_block, 0)
 
     def clear(w, _):
         acc[w] = jnp.zeros((144, 128), F32)

time: 45.6 us -> 45.6 us (level)
  no operation moved by 1% of the time
where the time goes in v6:
time: 45.6 us; the launch traced here: 45.5 us
  Pallas kernels  44.8 us (98%)
  between operations  0.66 us (1%)
    pallas_call x1, Pallas kernels, spectra(): pl.pallas_call(main_kernel, out_shape=(half, half), in_specs=[HBM_SPEC] *...  41 us
    pallas_call x1, Pallas kernels, mix(): pl.pallas_call(mix_kernel, out_shape=jax.ShapeDtypeStruct((2, 8, 512, 128...  3.86 us

profile of v6, /device:TPU:1, one launch (start us, length us, event | category | flops | bytes accessed | tf_op | source)
XLA Modules:
  0.0 45.5 jit_solution(4875733930819749894)
XLA Ops:
  0.7 41.0 %shard_map.64 = (bf16[512,1024]{1,0:T(8,128)(2,1)}, bf16[512,1024]{1,0:T(8,128)(2,1)}) custom-call(s32[1,512]{1,0:T(1,128)} %bitcast.4, s32[1,512]{1,0:T(1,128)} %bitcast.5, s32[1,1]{1,0:T(1,128)} %bitcast.3.cnt_hbm, bf16[512,1024]{1,0:T(8,128)(2,1)} %traces_hbm.1, bf16[4,256,512]{2,1,0:T(8,128)(2,1)} %constant.2.clone.table_hbm), custom_call_target="tpu_custom_call" | custom-call | tf_op jit(solution)/shard_map/pallas_call | solution.py:375
  41.6 3.9 %shard_map.65 = f32[2,8,512,128]{3,2,1,0:T(8,128)} custom-call(bf16[512,1024]{1,0:T(8,128)(2,1)} %get-tuple-element.7.own_ref, bf16[512,1024]{1,0:T(8,128)(2,1)} %get-tuple-element.8.other_ref, bf16[8,2,128,128]{3,2,1,0:T(8,128)(2,1)} %op_ref.1), custom_call_target="tpu_custom_call" | custom-call | tf_op jit(solution)/shard_map/pallas_call | solution.py:432
